TPU v7x, 32 devices: a whole 2x2x4 slice. The times are simulated.
32 devices in a mesh: dp: 8 (over z, x), mp: 4 (over y, core).
Axes of the slice: x: 2, y: 2, z: 4, core: 2. Of those that a mesh axis runs over, the one named last changes fastest.
Arguments:
- images: bfloat16 [2, 8, 608, 1024], P(None, 'dp', 'mp'), may hold values from -6 to 6
- counts: int32 [2, 8], P(None, 'dp'), may hold values from 0 to 1, as said below
- first_gain: bfloat16 [1024], P('dp'), may hold values from 0.5 to 1.5
- first_shift: bfloat16 [1024], P('dp'), may hold values from -1.796875 to 1.796875
- query_weight: bfloat16 [1024, 1024], P('dp', 'mp'), may hold values from -0.375 to 0.375
- query_bias: bfloat16 [4, 256], P('mp', 'dp'), may hold values from -3 to 3
- key_weight: bfloat16 [1024, 1024], P('dp', 'mp'), may hold values from -0.1875 to 0.1875
- value_weight: bfloat16 [1024, 1024], P('dp', 'mp'), may hold values from -0.1875 to 0.1875
- value_bias: bfloat16 [4, 256], P('mp', 'dp'), may hold values from -3 to 3
- out_weight: bfloat16 [1024, 1024], P('dp', 'mp'), may hold values from -1 to 1
- out_bias: bfloat16 [1024], P('dp'), may hold values from -1.796875 to 1.796875
- second_gain: bfloat16 [1024], P('dp'), may hold values from 0.5 to 1.5
- second_shift: bfloat16 [1024], P('dp'), may hold values from -1.796875 to 1.796875
- up_weight: bfloat16 [1024, 4096], P('dp', 'mp'), may hold values from -0.1875 to 0.1875
- up_bias: bfloat16 [4, 1024], P('mp', 'dp'), may hold values from -3 to 3
- down_weight: bfloat16 [1024, 4096], P('dp', 'mp'), may hold values from -0.09375 to 0.09375
- down_bias: bfloat16 [1024], P('dp'), may hold values from -1.796875 to 1.796875
- clip_tau: float32 [], replicated, may hold values from 3.5 to 5.5
- out_grad: bfloat16 [2, 8, 608, 1024], P(None, 'dp', 'mp'), may hold values from -6 to 6
Outputs:
- result: bfloat16 [2, 8, 608, 1024], P(None, 'dp', 'mp')
- input_grad: bfloat16 [2, 8, 608, 1024], P(None, 'dp', 'mp')
- first_gain_grad: float32 [1024], P('dp')
- first_shift_grad: float32 [1024], P('dp')
- query_weight_grad: float32 [1024, 1024], P('dp', 'mp')
- query_bias_grad: float32 [4, 256], P('mp', 'dp')
- key_weight_grad: float32 [1024, 1024], P('dp', 'mp')
- value_weight_grad: float32 [1024, 1024], P('dp', 'mp')
- value_bias_grad: float32 [4, 256], P('mp', 'dp')
- out_weight_grad: float32 [1024, 1024], P('dp', 'mp')
- out_bias_grad: float32 [1024], P('dp')
- second_gain_grad: float32 [1024], P('dp')
- second_shift_grad: float32 [1024], P('dp')
- up_weight_grad: float32 [1024, 4096], P('dp', 'mp')
- up_bias_grad: float32 [4, 1024], P('mp', 'dp')
- down_weight_grad: float32 [1024, 4096], P('dp', 'mp')
- down_bias_grad: float32 [1024], P('dp')
- logit_peaks: float32 [16], P('mp')
- clipped_query: float32 [1024, 1024], P('dp', 'mp')
- clipped_key: float32 [1024, 1024], P('dp', 'mp')
- clipped_bias: float32 [4, 256], P('mp', 'dp')
Inputs may be any that keep to these rules, and one draw needn't show every extreme that they name: The first counts[b, j] slots of index j hold images; in every micro-batch some index holds an image and some holds none.
All inputs are finite; a program needn't handle non-finite values.
Results may differ from a plain program's by a relative error of at most 0.012.
The roundings to bfloat16 on the way count: a program that leaves them out, or rounds other values in their place, can miss the bound.
Values may be sent and summed in bfloat16 or wider, within the bound.
A program may use at most 192 MiB of HBM per device.

v0:
```python
import math

import jax
import jax.numpy as jnp
from jax import lax
from jax.sharding import PartitionSpec as P

HD = 64
IMG_LEN = 577


def fetch_forward(
    query_weight,
    key_weight,
    value_weight,
    out_weight,
    up_weight,
    down_weight,
    first_gain,
    first_shift,
    out_bias,
    second_gain,
    second_shift,
    down_bias,
    query_bias,
    value_bias,
    up_bias,
):
    return (
        lax.all_gather(query_weight, "dp", axis=0, tiled=True),
        lax.all_gather(key_weight, "dp", axis=0, tiled=True),
        lax.all_gather(value_weight, "dp", axis=0, tiled=True),
        lax.all_gather(out_weight, "dp", axis=0, tiled=True),
        lax.all_gather(up_weight, "dp", axis=0, tiled=True),
        lax.all_gather(down_weight, "dp", axis=0, tiled=True),
        lax.all_gather(first_gain, "dp", axis=0, tiled=True),
        lax.all_gather(first_shift, "dp", axis=0, tiled=True),
        lax.all_gather(out_bias, "dp", axis=0, tiled=True),
        lax.all_gather(second_gain, "dp", axis=0, tiled=True),
        lax.all_gather(second_shift, "dp", axis=0, tiled=True),
        lax.all_gather(down_bias, "dp", axis=0, tiled=True),
        lax.all_gather(query_bias, "dp", axis=1, tiled=True),
        lax.all_gather(value_bias, "dp", axis=1, tiled=True),
        lax.all_gather(up_bias, "dp", axis=1, tiled=True),
    )


def fetch_backward(
    query_weight,
    key_weight,
    value_weight,
    out_weight,
    up_weight,
    down_weight,
    first_gain,
    first_shift,
    out_bias,
    second_gain,
    second_shift,
    down_bias,
    query_bias,
    value_bias,
    up_bias,
):
    return (
        lax.all_gather(query_weight, "dp", axis=0, tiled=True),
        lax.all_gather(key_weight, "dp", axis=0, tiled=True),
        lax.all_gather(value_weight, "dp", axis=0, tiled=True),
        lax.all_gather(out_weight, "dp", axis=0, tiled=True),
        lax.all_gather(up_weight, "dp", axis=0, tiled=True),
        lax.all_gather(down_weight, "dp", axis=0, tiled=True),
        lax.all_gather(first_gain, "dp", axis=0, tiled=True),
        lax.all_gather(first_shift, "dp", axis=0, tiled=True),
        lax.all_gather(out_bias, "dp", axis=0, tiled=True),
        lax.all_gather(second_gain, "dp", axis=0, tiled=True),
        lax.all_gather(second_shift, "dp", axis=0, tiled=True),
        lax.all_gather(down_bias, "dp", axis=0, tiled=True),
        lax.all_gather(query_bias, "dp", axis=1, tiled=True),
        lax.all_gather(value_bias, "dp", axis=1, tiled=True),
        lax.all_gather(up_bias, "dp", axis=1, tiled=True),
    )


def spread_normed(rows_low):
    return lax.all_gather(rows_low, "mp", axis=1, tiled=True)


def collect_branch(partial_rows):
    return lax.psum_scatter(partial_rows, "mp", scatter_dimension=1, tiled=True)


def spread_grads(rows_low):
    return lax.all_gather(rows_low, "mp", axis=1, tiled=True)


def collect_normed(partial_rows):
    return lax.psum_scatter(partial_rows, "mp", scatter_dimension=1, tiled=True)


def standardize_rows(features):
    center = features - jnp.mean(features, axis=-1, keepdims=True)
    inverse_deviation = lax.rsqrt(jnp.mean(center * center, axis=-1, keepdims=True) + 1e-05)
    return (center * inverse_deviation, inverse_deviation)


def layer_norm_backward(incoming_gradient, centered_scaled, inverse_deviation, norm_gain):
    upward_scaled = incoming_gradient * norm_gain
    return inverse_deviation * (
        upward_scaled
        - jnp.mean(upward_scaled, axis=-1, keepdims=True)
        - centered_scaled * jnp.mean(upward_scaled * centered_scaled, axis=-1, keepdims=True)
    )


def row_sum(rows_low):
    return jnp.sum(rows_low.astype(jnp.float32), axis=(0, 1))


def on_device(
    images,
    counts,
    first_gain,
    first_shift,
    query_weight,
    query_bias,
    key_weight,
    value_weight,
    value_bias,
    out_weight,
    out_bias,
    second_gain,
    second_shift,
    up_weight,
    up_bias,
    down_weight,
    down_bias,
    clip_tau,
    out_grad,
):
    batches, slots, part_rows, model_width = images.shape
    group_size = lax.axis_size("mp")
    full_rows = part_rows * group_size
    mp_at = lax.axis_index("mp")
    dp_at = lax.axis_index("dp")
    row_start = mp_at * part_rows
    local_width = query_weight.shape[1]
    local_units = up_weight.shape[1]
    heads_here = local_width // HD
    score_scale = 1.0 / math.sqrt(HD)
    key_keep = jnp.arange(full_rows) < IMG_LEN
    part_keep = row_start + jnp.arange(part_rows) < IMG_LEN
    single_float = jnp.float32
    brain_float_half = jnp.bfloat16
    grad_query = jnp.zeros((model_width, local_width), single_float)
    grad_key = jnp.zeros((model_width, local_width), single_float)
    grad_value = jnp.zeros((model_width, local_width), single_float)
    grad_out = jnp.zeros((model_width, local_width), single_float)
    grad_up = jnp.zeros((model_width, local_units), single_float)
    grad_down = jnp.zeros((model_width, local_units), single_float)
    grad_qbias = jnp.zeros((local_width,), single_float)
    grad_vbias = jnp.zeros((local_width,), single_float)
    grad_ubias = jnp.zeros((local_units,), single_float)
    first_norm_gain_gradient = jnp.zeros((model_width,), single_float)
    grad_shift_one = jnp.zeros((model_width,), single_float)
    grad_obias = jnp.zeros((model_width,), single_float)
    second_norm_gain_gradient = jnp.zeros((model_width,), single_float)
    grad_shift_two = jnp.zeros((model_width,), single_float)
    grad_dbias = jnp.zeros((model_width,), single_float)
    peak_now = jnp.full((heads_here,), -1e30, single_float)
    result_list = []
    input_list = []

    def scores_of(query_heads, key_heads):
        return (
            jnp.einsum(
                "sqhc,skhc->shqk", query_heads, key_heads, preferred_element_type=single_float
            )
            * score_scale
        )

    for micro_at in range(batches):
        gathered = fetch_forward(
            query_weight,
            key_weight,
            value_weight,
            out_weight,
            up_weight,
            down_weight,
            first_gain,
            first_shift,
            out_bias,
            second_gain,
            second_shift,
            down_bias,
            query_bias,
            value_bias,
            up_bias,
        )
        (
            query_full,
            key_full,
            value_full,
            out_full,
            up_full,
            down_full,
            first_norm_gain,
            first_norm_shift,
            obias_full,
            second_norm_gain,
            second_norm_shift,
            dbias_full,
            qbias_full,
            vbias_full,
            ubias_full,
        ) = gathered
        live_slots = jnp.arange(slots) < counts[micro_at, 0]
        local_mask = (live_slots[:, None] & part_keep[None, :]).astype(single_float)[..., None]
        picture_rows = images[micro_at].astype(single_float)
        first_centered_scaled, first_inverse_deviation = standardize_rows(picture_rows)
        normed_one = spread_normed(
            (
                first_centered_scaled * first_norm_gain.astype(single_float)
                + first_norm_shift.astype(single_float)
            ).astype(brain_float_half)
        )
        queries = (
            jnp.einsum("spd,de->spe", normed_one, query_full, preferred_element_type=single_float)
            + qbias_full.reshape(-1).astype(single_float)
        ).astype(brain_float_half)
        key_rows = jnp.einsum(
            "spd,de->spe", normed_one, key_full, preferred_element_type=single_float
        ).astype(brain_float_half)
        value_rows = (
            jnp.einsum("spd,de->spe", normed_one, value_full, preferred_element_type=single_float)
            + vbias_full.reshape(-1).astype(single_float)
        ).astype(brain_float_half)
        query_heads = queries.reshape(slots, full_rows, heads_here, HD)
        key_heads = key_rows.reshape(slots, full_rows, heads_here, HD)
        value_heads = value_rows.reshape(slots, full_rows, heads_here, HD)
        raw_scores = scores_of(query_heads, key_heads)
        valid_pairs = (
            live_slots[:, None, None, None]
            & key_keep[None, None, :, None]
            & key_keep[None, None, None, :]
        )
        peak_micro = jnp.max(jnp.where(valid_pairs, raw_scores, -1e30), axis=(0, 2, 3))
        peak_now = jnp.maximum(peak_now, lax.pmax(peak_micro, "dp"))
        masked = jnp.where(key_keep[None, None, None, :], raw_scores, -1e30)
        row_top = jnp.max(masked, axis=-1, keepdims=True)
        expo = jnp.exp(masked - row_top)
        row_total = jnp.sum(expo, axis=-1, keepdims=True)
        log_total = row_top + jnp.log(row_total)
        probs_low = (expo / row_total).astype(brain_float_half)
        mixed = (
            jnp.einsum(
                "shqk,skhc->sqhc", probs_low, value_heads, preferred_element_type=single_float
            )
            .reshape(slots, full_rows, local_width)
            .astype(brain_float_half)
        )
        attn_part = jnp.einsum("spe,de->spd", mixed, out_full, preferred_element_type=single_float)
        attended = collect_branch(attn_part)
        after_attention_rows = picture_rows + attended + obias_full.astype(single_float)
        second_centered_scaled, second_inverse_deviation = standardize_rows(after_attention_rows)
        normed_two = spread_normed(
            (
                second_centered_scaled * second_norm_gain.astype(single_float)
                + second_norm_shift.astype(single_float)
            ).astype(brain_float_half)
        )
        hidden_pre = jnp.einsum(
            "spd,df->spf", normed_two, up_full, preferred_element_type=single_float
        ) + ubias_full.reshape(-1).astype(single_float)
        sigmoid_part = jax.nn.sigmoid(1.702 * hidden_pre)
        activated = (hidden_pre * sigmoid_part).astype(brain_float_half)
        projected = collect_branch(
            jnp.einsum("spf,df->spd", activated, down_full, preferred_element_type=single_float)
        )
        output_rows = local_mask * (
            after_attention_rows + projected + dbias_full.astype(single_float)
        )
        result_list.append(output_rows.astype(brain_float_half))
        regathered = fetch_backward(
            query_weight,
            key_weight,
            value_weight,
            out_weight,
            up_weight,
            down_weight,
            first_gain,
            first_shift,
            out_bias,
            second_gain,
            second_shift,
            down_bias,
            query_bias,
            value_bias,
            up_bias,
        )
        (
            query_back_w,
            key_back_w,
            value_back_w,
            out_back_w,
            up_back_w,
            down_back_w,
            first_norm_gain_row,
            shift_one_b,
            obias_back,
            second_norm_gain_row,
            shift_two_b,
            dbias_back,
            qbias_back,
            vbias_back,
            ubias_back,
        ) = regathered
        out_back = out_grad[micro_at].astype(single_float) * local_mask
        proj_back = out_back.astype(brain_float_half)
        grad_dbias = grad_dbias + row_sum(proj_back)
        proj_full = spread_grads(proj_back)
        grad_down = grad_down + jnp.einsum(
            "spd,spf->df", proj_full, activated, preferred_element_type=single_float
        )
        act_back = jnp.einsum(
            "spd,df->spf", proj_full, down_back_w, preferred_element_type=single_float
        )
        pre_back = (
            act_back * (sigmoid_part + 1.702 * hidden_pre * sigmoid_part * (1.0 - sigmoid_part))
        ).astype(brain_float_half)
        grad_ubias = grad_ubias + row_sum(pre_back)
        grad_up = grad_up + jnp.einsum(
            "spd,spf->df", normed_two, pre_back, preferred_element_type=single_float
        )
        norm_two_part = jnp.einsum(
            "spf,df->spd", pre_back, up_back_w, preferred_element_type=single_float
        )
        second_norm_backward = collect_normed(norm_two_part)
        attn_back = out_back + layer_norm_backward(
            second_norm_backward,
            second_centered_scaled,
            second_inverse_deviation,
            second_norm_gain_row.astype(single_float),
        )
        attended_back = attn_back.astype(brain_float_half)
        grad_obias = grad_obias + row_sum(attended_back)
        attended_full = spread_grads(attended_back)
        second_norm_gain_gradient = second_norm_gain_gradient + jnp.sum(
            second_norm_backward * second_centered_scaled, axis=(0, 1)
        )
        grad_shift_two = grad_shift_two + jnp.sum(second_norm_backward, axis=(0, 1))
        grad_out = grad_out + jnp.einsum(
            "spd,spe->de", attended_full, mixed, preferred_element_type=single_float
        )
        mixed_back = (
            jnp.einsum(
                "spd,de->spe", attended_full, out_back_w, preferred_element_type=single_float
            )
            .astype(brain_float_half)
            .reshape(slots, full_rows, heads_here, HD)
        )
        again_scores = jnp.where(
            key_keep[None, None, None, :], scores_of(query_heads, key_heads), -1e30
        )
        probs_again = jnp.exp(again_scores - log_total)
        value_back = (
            jnp.einsum(
                "shqk,sqhc->skhc",
                probs_again.astype(brain_float_half),
                mixed_back,
                preferred_element_type=single_float,
            )
            .astype(brain_float_half)
            .reshape(slots, full_rows, local_width)
        )
        prob_back = jnp.einsum(
            "sqhc,skhc->shqk", mixed_back, value_heads, preferred_element_type=single_float
        )
        score_back = (
            probs_again * (prob_back - jnp.sum(prob_back * probs_again, axis=-1, keepdims=True))
        ).astype(brain_float_half)
        query_back = (
            (
                jnp.einsum(
                    "shqk,skhc->sqhc", score_back, key_heads, preferred_element_type=single_float
                )
                * score_scale
            )
            .astype(brain_float_half)
            .reshape(slots, full_rows, local_width)
        )
        key_back = (
            (
                jnp.einsum(
                    "shqk,sqhc->skhc", score_back, query_heads, preferred_element_type=single_float
                )
                * score_scale
            )
            .astype(brain_float_half)
            .reshape(slots, full_rows, local_width)
        )
        grad_query = grad_query + jnp.einsum(
            "spd,spe->de", normed_one, query_back, preferred_element_type=single_float
        )
        grad_key = grad_key + jnp.einsum(
            "spd,spe->de", normed_one, key_back, preferred_element_type=single_float
        )
        grad_value = grad_value + jnp.einsum(
            "spd,spe->de", normed_one, value_back, preferred_element_type=single_float
        )
        grad_qbias = grad_qbias + row_sum(query_back)
        grad_vbias = grad_vbias + row_sum(value_back)
        norm_one_part = (
            jnp.einsum("spe,de->spd", query_back, query_back_w, preferred_element_type=single_float)
            + jnp.einsum("spe,de->spd", key_back, key_back_w, preferred_element_type=single_float)
            + jnp.einsum(
                "spe,de->spd", value_back, value_back_w, preferred_element_type=single_float
            )
        )
        first_norm_backward = collect_normed(norm_one_part)
        first_norm_gain_gradient = first_norm_gain_gradient + jnp.sum(
            first_norm_backward * first_centered_scaled, axis=(0, 1)
        )
        grad_shift_one = grad_shift_one + jnp.sum(first_norm_backward, axis=(0, 1))
        rows_back = attn_back + layer_norm_backward(
            first_norm_backward,
            first_centered_scaled,
            first_inverse_deviation,
            first_norm_gain_row.astype(single_float),
        )
        input_list.append(rows_back.astype(brain_float_half))
    vector_grads = lax.psum(
        (
            first_norm_gain_gradient,
            grad_shift_one,
            grad_obias,
            second_norm_gain_gradient,
            grad_shift_two,
            grad_dbias,
        ),
        "mp",
    )
    summed = (
        lax.psum_scatter(grad_query, "dp", scatter_dimension=0, tiled=True),
        lax.psum_scatter(grad_key, "dp", scatter_dimension=0, tiled=True),
        lax.psum_scatter(grad_value, "dp", scatter_dimension=0, tiled=True),
        lax.psum_scatter(grad_out, "dp", scatter_dimension=0, tiled=True),
        lax.psum_scatter(grad_up, "dp", scatter_dimension=0, tiled=True),
        lax.psum_scatter(grad_down, "dp", scatter_dimension=0, tiled=True),
        lax.psum_scatter(vector_grads[0], "dp", scatter_dimension=0, tiled=True),
        lax.psum_scatter(vector_grads[1], "dp", scatter_dimension=0, tiled=True),
        lax.psum_scatter(vector_grads[2], "dp", scatter_dimension=0, tiled=True),
        lax.psum_scatter(vector_grads[3], "dp", scatter_dimension=0, tiled=True),
        lax.psum_scatter(vector_grads[4], "dp", scatter_dimension=0, tiled=True),
        lax.psum_scatter(vector_grads[5], "dp", scatter_dimension=0, tiled=True),
        lax.psum_scatter(grad_qbias.reshape(1, local_width), "dp", scatter_dimension=1, tiled=True),
        lax.psum_scatter(grad_vbias.reshape(1, local_width), "dp", scatter_dimension=1, tiled=True),
        lax.psum_scatter(grad_ubias.reshape(1, local_units), "dp", scatter_dimension=1, tiled=True),
    )
    head_root = jnp.sqrt(clip_tau / jnp.maximum(peak_now, clip_tau))
    column_root = jnp.repeat(head_root, HD)
    clipped_query = query_weight.astype(single_float) * column_root[None, :]
    clipped_key = key_weight.astype(single_float) * column_root[None, :]
    bias_cols = query_bias.shape[1]
    column_head = (dp_at * bias_cols + jnp.arange(bias_cols)) // HD
    head_match = (column_head[:, None] == jnp.arange(heads_here)[None, :]).astype(single_float)
    bias_factor = jnp.sum(head_match * head_root[None, :], axis=1)
    clipped_bias = query_bias.astype(single_float) * bias_factor[None, :]
    return (
        jnp.stack(result_list),
        jnp.stack(input_list),
        summed[6],
        summed[7],
        summed[0],
        summed[12],
        summed[1],
        summed[2],
        summed[13],
        summed[3],
        summed[8],
        summed[9],
        summed[10],
        summed[4],
        summed[14],
        summed[5],
        summed[11],
        peak_now,
        clipped_query,
        clipped_key,
        clipped_bias,
    )


def solution(mesh):
    return jax.shard_map(
        on_device,
        mesh=mesh,
        in_specs=(
            P(None, "dp", "mp", None),
            P(None, "dp"),
            P("dp"),
            P("dp"),
            P("dp", "mp"),
            P("mp", "dp"),
            P("dp", "mp"),
            P("dp", "mp"),
            P("mp", "dp"),
            P("dp", "mp"),
            P("dp"),
            P("dp"),
            P("dp"),
            P("dp", "mp"),
            P("mp", "dp"),
            P("dp", "mp"),
            P("dp"),
            P(),
            P(None, "dp", "mp", None),
        ),
        out_specs=(
            P(None, "dp", "mp", None),
            P(None, "dp", "mp", None),
            P("dp"),
            P("dp"),
            P("dp", "mp"),
            P("mp", "dp"),
            P("dp", "mp"),
            P("dp", "mp"),
            P("mp", "dp"),
            P("dp", "mp"),
            P("dp"),
            P("dp"),
            P("dp"),
            P("dp", "mp"),
            P("mp", "dp"),
            P("dp", "mp"),
            P("dp"),
            P("mp"),
            P("dp", "mp"),
            P("dp", "mp"),
            P("mp", "dp"),
        ),
        check_vma=False,
    )
```

profile of v0, /device:TPU:0, one launch (start us, length us, event | category | flops | bytes accessed | tf_op | source)
XLA Modules:
  0.0 1390.1 jit_solution(16776261457515294469)
XLA Ops:
  10.9 22.3 %all-gather = bf16[8,1,128]{2,1,0:T(2,128)(2,1)S(1)} all-gather(bf16[1,1,128]{2,1,0:T(2,128)(2,1)} %bitcast.405), channel_id=1, replica_groups=mesh['dp'=8,'mp'=4] {'dp'}, dimensions={0}, use_global_device_ids=true | all-gather | bytes 2304 | tf_op jit(solution)/shard_map/all_gather | solution.py:36
  33.2 16.4 %all-gather.1 = bf16[8,1,128]{2,1,0:T(2,128)(2,1)S(1)} all-gather(bf16[1,1,128]{2,1,0:T(2,128)(2,1)} %bitcast.406), channel_id=1, replica_groups=mesh['dp'=8,'mp'=4] {'dp'}, dimensions={0}, use_global_device_ids=true | all-gather | bytes 2304 | tf_op jit(solution)/shard_map/all_gather | solution.py:37
  49.6 2.2 fusion.110
  54.4 19.0 %all-reduce.11 = (bf16[256]{0:T(256)(128)(2,1)S(1)}, bf16[256]{0:T(256)(128)(2,1)S(1)}) all-reduce(bf16[256]{0:T(256)(128)(2,1)S(1)} %dynamic-update-slice, bf16[256]{0:T(256)(128)(2,1)S(1)} %dynamic-update-slice.1), channel_id=1, replica_groups=mesh['dp'=8,'mp'=4] {'dp'}, use_global_device_ids=true, to_apply=%add | all-reduce | flops 512 | bytes 2048
  75.4 31.4 %all_gather.49 = bf16[1024,256]{1,0:T(8,128)(2,1)S(1)} all-gather(bf16[128,256]{1,0:T(8,128)(2,1)S(1)} %copy-done.48), channel_id=1, replica_groups=mesh['dp'=8,'mp'=4] {'dp'}, dimensions={0}, use_global_device_ids=true | all-gather | bytes 589824 | tf_op jit(solution)/shard_map/all_gather | solution.py:32
  106.8 33.5 %all_gather.108 = bf16[1024,256]{1,0:T(8,128)(2,1)} all-gather(bf16[128,256]{1,0:T(8,128)(2,1)S(1)} %copy-done.49), channel_id=1, replica_groups=mesh['dp'=8,'mp'=4] {'dp'}, dimensions={0}, use_global_device_ids=true | all-gather | bytes 589824 | tf_op jit(solution)/shard_map/all_gather | solution.py:33
  140.3 31.6 %all_gather.51 = bf16[1024,256]{1,0:T(8,128)(2,1)S(1)} all-gather(bf16[128,256]{1,0:T(8,128)(2,1)S(1)} %copy-done.45), channel_id=1, replica_groups=mesh['dp'=8,'mp'=4] {'dp'}, dimensions={0}, use_global_device_ids=true | all-gather | bytes 589824 | tf_op jit(solution)/shard_map/all_gather | solution.py:30
  171.9 33.2 %all_gather.53 = bf16[1024,256]{1,0:T(8,128)(2,1)} all-gather(bf16[128,256]{1,0:T(8,128)(2,1)S(1)} %copy-done.47), channel_id=1, replica_groups=mesh['dp'=8,'mp'=4] {'dp'}, dimensions={0}, use_global_device_ids=true | all-gather | bytes 589824 | tf_op jit(solution)/shard_map/all_gather | solution.py:31
  209.1 2.7 fusion.75
  213.1 2.4 fusion.63
  220.4 5.7 select_reduce_fusion.1
  231.3 16.5 %all-gather.2 = bf16[8,1,128]{2,1,0:T(2,128)(2,1)S(1)} all-gather(bf16[1,1,128]{2,1,0:T(2,128)(2,1)S(1)} %bitcast.407), channel_id=1, replica_groups=mesh['dp'=8,'mp'=4] {'dp'}, dimensions={0}, use_global_device_ids=true | all-gather | bytes 2304 | tf_op jit(solution)/shard_map/all_gather | solution.py:38
  247.9 17.9 %all-gather.3 = bf16[8,1,128]{2,1,0:T(2,128)(2,1)S(1)} all-gather(bf16[1,1,128]{2,1,0:T(2,128)(2,1)S(1)} %bitcast.408), channel_id=1, replica_groups=mesh['dp'=8,'mp'=4] {'dp'}, dimensions={0}, use_global_device_ids=true | all-gather | bytes 2304 | tf_op jit(solution)/shard_map/all_gather | solution.py:39
  265.8 17.0 %all-gather.4 = bf16[8,1,128]{2,1,0:T(2,128)(2,1)S(1)} all-gather(bf16[1,1,128]{2,1,0:T(2,128)(2,1)S(1)} %bitcast.409), channel_id=1, replica_groups=mesh['dp'=8,'mp'=4] {'dp'}, dimensions={0}, use_global_device_ids=true | all-gather | bytes 2304 | tf_op jit(solution)/shard_map/all_gather | solution.py:40
  287.0 17.7 %all_gather.114 = bf16[1,1024]{1,0:T(2,128)(2,1)S(1)} all-gather(bf16[1,128]{1,0:T(2,128)(2,1)S(1)} %copy-done.84), channel_id=1, replica_groups=mesh['dp'=8,'mp'=4] {'dp'}, dimensions={1}, use_global_device_ids=true | all-gather | bytes 2304 | tf_op jit(solution)/shard_map/all_gather | solution.py:44
  304.7 5.0 fusion.36
  309.7 10.7 all-gather.29.cloned.1.call-done
  320.3 51.7 %all-gather.23.cloned.1.call-done = bf16[1024,1024]{1,0:T(8,128)(2,1)} async-done(((bf16[128,1024]{1,0:T(8,128)(2,1)}), bf16[1024,1024]{1,0:T(8,128)(2,1)}) %all-gather.23.cloned.1.call-update) | async-done | bytes 2097168 | tf_op jit(solution)/shard_map/all_gather | solution.py:35
  372.1 5.6 convert_reduce_fusion.1
  377.7 2.9 convolution_bitcast_fusion.1
  380.7 5.3 convolution_bitcast_fusion.3
  386.6 17.9 %all-gather.5 = bf16[8,1,128]{2,1,0:T(2,128)(2,1)S(1)} all-gather(bf16[1,1,128]{2,1,0:T(2,128)(2,1)S(1)} %bitcast.410), channel_id=1, replica_groups=mesh['dp'=8,'mp'=4] {'dp'}, dimensions={0}, use_global_device_ids=true | all-gather | bytes 2304 | tf_op jit(solution)/shard_map/all_gather | solution.py:41
  404.6 8.5 reduce-scatter.32.cloned.1.call-done
  415.1 34.3 %reduce-scatter.26.cloned.1.call-done = f32[1,152,1024]{2,1,0:T(8,128)} async-done(((f32[1,608,1024]{2,1,0:T(8,128)}), f32[1,152,1024]{2,1,0:T(8,128)}) %reduce-scatter.26.cloned.1.call-update) | async-done | bytes 622608 | tf_op jit(solution)/shard_map/reduce_scatter | solution.py:89
  449.4 3.6 convert_reduce_fusion.11
  454.1 16.7 %all-gather.31.cloned.1.call-done = bf16[1,608,1024]{2,1,0:T(8,128)(2,1)} async-done(((bf16[1,152,1024]{2,1,0:T(8,128)(2,1)}), bf16[1,608,1024]{2,1,0:T(8,128)(2,1)}) %all-gather.31.cloned.1.call-update) | async-done | bytes 1245200 | tf_op jit(solution)/shard_map/all_gather | solution.py:93
  470.9 2.8 fusion.66
  474.8 12.6 select_reduce_fusion
  492.1 33.8 %reduce-scatter.28.cloned.1.call-done = f32[1,152,1024]{2,1,0:T(8,128)} async-done(((f32[1,608,1024]{2,1,0:T(8,128)}), f32[1,152,1024]{2,1,0:T(8,128)}) %reduce-scatter.28.cloned.1.call-update) | async-done | bytes 622608 | tf_op jit(solution)/shard_map/reduce_scatter | solution.py:89
  529.5 16.7 %all-gather.27.cloned.1.call-done = bf16[1,608,1024]{2,1,0:T(8,128)(2,1)} async-done(((bf16[1,152,1024]{2,1,0:T(8,128)(2,1)}), bf16[1,608,1024]{2,1,0:T(8,128)(2,1)}) %all-gather.27.cloned.1.call-update) | async-done | bytes 1245200 | tf_op jit(solution)/shard_map/all_gather | solution.py:85
  546.1 5.0 fusion.25
  551.1 14.1 %all-gather.33.cloned.1.call-done = bf16[1,608,1024]{2,1,0:T(8,128)(2,1)} async-done(((bf16[1,152,1024]{2,1,0:T(8,128)(2,1)}), bf16[1,608,1024]{2,1,0:T(8,128)(2,1)}) %all-gather.33.cloned.1.call-update) | async-done | bytes 1245200 | tf_op jit(solution)/shard_map/all_gather | solution.py:93
  565.3 5.0 convert_reduce_fusion
  570.3 2.9 convolution_bitcast_fusion
  573.3 5.3 convolution_bitcast_fusion.2
  578.7 28.5 %reduce-scatter.36.cloned.1.call-done = f32[1,152,1024]{2,1,0:T(8,128)} async-done(((f32[1,608,1024]{2,1,0:T(8,128)}), f32[1,152,1024]{2,1,0:T(8,128)}) %reduce-scatter.36.cloned.1.call-update) | async-done | bytes 622608 | tf_op jit(solution)/shard_map/reduce_scatter | solution.py:97
  608.7 35.2 %reduce-scatter.30.cloned.1.call-done = f32[1,152,1024]{2,1,0:T(8,128)} async-done(((f32[1,608,1024]{2,1,0:T(8,128)}), f32[1,152,1024]{2,1,0:T(8,128)}) %reduce-scatter.30.cloned.1.call-update) | async-done | bytes 622608 | tf_op jit(solution)/shard_map/reduce_scatter | solution.py:89
  643.9 3.3 convert_reduce_fusion.10
  647.3 5.7 convert_reduce_fusion.5
  654.3 10.7 all-gather.35.cloned.1.call-done
  667.0 5.2 convert_reduce_fusion.4
  672.3 7.5 multiply_reduce_fusion
  679.8 6.9 multiply_convert_fusion.1
  693.1 3.1 fusion.145
  697.1 4.9 add_bitcast_fusion
  709.7 3.8 fusion.21
  713.5 4.0 convolution_add_fusion
  717.6 3.7 fusion.34
  721.4 4.0 convolution_add_fusion.1
  728.3 3.0 convolution_add_fusion.2
  732.5 2.6 convolution_add_fusion.3
  740.0 21.6 %all-reduce.9 = (f32[4]{0:T(128)S(1)}, f32[4]{0:T(128)S(1)}) all-reduce(f32[4]{0:T(128)S(1)} %copy-done.95, f32[4]{0:T(128)S(1)} %copy-done.94), channel_id=1, replica_groups=mesh['dp'=8,'mp'=4] {'dp'}, use_global_device_ids=true, to_apply=%region_72.73 | all-reduce | flops 8 | bytes 64 | tf_op jit(solution)/shard_map/pmax | solution.py:247
  772.0 22.5 %reduce-scatter.54.cloned.1.call-done = f32[32,1]{1,0:T(8,128)} async-done(((f32[256,1]{1,0:T(8,128)}), f32[32,1]{1,0:T(8,128)}) %reduce-scatter.54.cloned.1.call-update) | async-done | bytes 144
  795.8 62.4 %reduce-scatter.52.cloned.1.call-done = f32[32,1]{1,0:T(8,128)} async-done(((f32[256,1]{1,0:T(8,128)}), f32[32,1]{1,0:T(8,128)}) %reduce-scatter.52.cloned.1.call-update) | async-done | bytes 144
  859.5 34.1 %reduce-scatter.38.cloned.1.call-done = f32[1,152,1024]{2,1,0:T(8,128)} async-done(((f32[1,608,1024]{2,1,0:T(8,128)}), f32[1,152,1024]{2,1,0:T(8,128)}) %reduce-scatter.38.cloned.1.call-update) | async-done | bytes 622608 | tf_op jit(solution)/shard_map/reduce_scatter | solution.py:97
  893.7 36.4 %reduce-scatter.34.cloned.1.call-done = f32[1,152,1024]{2,1,0:T(8,128)} async-done(((f32[1,608,1024]{2,1,0:T(8,128)}), f32[1,152,1024]{2,1,0:T(8,128)}) %reduce-scatter.34.cloned.1.call-update) | async-done | bytes 622608 | tf_op jit(solution)/shard_map/reduce_scatter | solution.py:97
  932.0 38.4 %all-reduce.8 = (f32[1024]{0:T(1024)S(1)}, f32[1024]{0:T(1024)S(1)}, f32[1024]{0:T(1024)S(1)}, f32[1024]{0:T(1024)S(1)}, f32[1024]{0:T(1024)S(1)}, /*index=5*/f32[1024]{0:T(1024)S(1)}) all-reduce(f32[1024]{0:T(1024)S(1)} %add.438, f32[1024]{0:T(1024)S(1)} %add.439, ...), channel_id=10, replica_groups=mesh['dp'=8,'mp'=4] {'dp'}, use_global_device_ids=true, to_apply=%region_33.34.clone | all-reduce | flops 6144 | bytes 49152
  970.8 6.6 all-reduce.10
  980.0 42.9 %reduce-scatter.50.cloned.1.call-done = f32[128,1024]{1,0:T(8,128)} async-done(((f32[1024,1024]{1,0:T(8,128)}), f32[128,1024]{1,0:T(8,128)}) %reduce-scatter.50.cloned.1.call-update) | async-done | bytes 524304 | tf_op jit(solution)/shard_map/reduce_scatter | solution.py:448
  1023.0 91.7 %reduce-scatter.48.cloned.1.call-done = f32[128,1024]{1,0:T(8,128)} async-done(((f32[1024,1024]{1,0:T(8,128)}), f32[128,1024]{1,0:T(8,128)}) %reduce-scatter.48.cloned.1.call-update) | async-done | bytes 524304 | tf_op jit(solution)/shard_map/reduce_scatter | solution.py:447
  1114.7 67.6 %reduce-scatter.46.cloned.1.call-done = f32[128,256]{1,0:T(8,128)} async-done(((f32[1024,256]{1,0:T(8,128)}), f32[128,256]{1,0:T(8,128)}) %reduce-scatter.46.cloned.1.call-update) | async-done | bytes 131088 | tf_op jit(solution)/shard_map/reduce_scatter | solution.py:446
  1182.3 66.5 %reduce-scatter.44.cloned.1.call-done = f32[128,256]{1,0:T(8,128)} async-done(((f32[1024,256]{1,0:T(8,128)}), f32[128,256]{1,0:T(8,128)}) %reduce-scatter.44.cloned.1.call-update) | async-done | bytes 131088 | tf_op jit(solution)/shard_map/reduce_scatter | solution.py:445
  1248.8 66.7 %reduce-scatter.40.cloned.1.call-done = f32[128,256]{1,0:T(8,128)} async-done(((f32[1024,256]{1,0:T(8,128)}), f32[128,256]{1,0:T(8,128)}) %reduce-scatter.40.cloned.1.call-update) | async-done | bytes 131088 | tf_op jit(solution)/shard_map/reduce_scatter | solution.py:443
  1315.6 66.7 %reduce-scatter.42.cloned.1.call-done = f32[128,256]{1,0:T(8,128)} async-done(((f32[1024,256]{1,0:T(8,128)}), f32[128,256]{1,0:T(8,128)}) %reduce-scatter.42.cloned.1.call-update) | async-done | bytes 131088 | tf_op jit(solution)/shard_map/reduce_scatter | solution.py:444
  (383 shorter events, 83.1 us)
Async XLA Ops:
  8.0 44.6 %copy-start.79 = (u32[32]{0:T(128)S(1)}, u32[32]{0:T(128)}, u32[]{:S(2)}) copy-start(u32[32]{0:T(128)} %constant.79) | copy-start | bytes 388
  8.0 45.9 %copy-start.90 = (bf16[1,32]{1,0:T(2,128)(2,1)S(1)}, bf16[1,32]{1,0:T(2,128)(2,1)}, u32[]{:S(2)}) copy-start(bf16[1,32]{1,0:T(2,128)(2,1)} %param.27) | copy-start | bytes 196
  8.0 46.1 %copy-start.91 = (bf16[1,32]{1,0:T(2,128)(2,1)S(1)}, bf16[1,32]{1,0:T(2,128)(2,1)}, u32[]{:S(2)}) copy-start(bf16[1,32]{1,0:T(2,128)(2,1)} %param.24) | copy-start | bytes 196
  8.1 65.4 %copy-start.80 = (s32[2,1]{0,1:T(1,128)S(1)}, s32[2,1]{0,1:T(1,128)}, u32[]{:S(2)}) copy-start(s32[2,1]{0,1:T(1,128)} %param.20) | copy-start | bytes 28
  8.1 67.3 %copy-start.48 = (bf16[128,256]{1,0:T(8,128)(2,1)S(1)}, bf16[128,256]{1,0:T(8,128)(2,1)}, u32[]{:S(2)}) copy-start(bf16[128,256]{1,0:T(8,128)(2,1)} %param.26) | copy-start | bytes 196612
  8.1 98.7 %copy-start.49 = (bf16[128,256]{1,0:T(8,128)(2,1)S(1)}, bf16[128,256]{1,0:T(8,128)(2,1)}, u32[]{:S(2)}) copy-start(bf16[128,256]{1,0:T(8,128)(2,1)} %param.28) | copy-start | bytes 196612
  8.1 132.2 %copy-start.45 = (bf16[128,256]{1,0:T(8,128)(2,1)S(1)}, bf16[128,256]{1,0:T(8,128)(2,1)}, u32[]{:S(2)}) copy-start(bf16[128,256]{1,0:T(8,128)(2,1)} %param.23) | copy-start | bytes 196612
  8.1 163.8 %copy-start.47 = (bf16[128,256]{1,0:T(8,128)(2,1)S(1)}, bf16[128,256]{1,0:T(8,128)(2,1)}, u32[]{:S(2)}) copy-start(bf16[128,256]{1,0:T(8,128)(2,1)} %param.25) | copy-start | bytes 196612
  8.1 198.2 %all-gather.25.cloned.1.call-start = ((), (), s32[]{:S(2)}) async-start(), calls=%async_computation.23 | async-start | bytes 1556480 | tf_op jit(solution)/shard_map/all_gather | solution.py:85
  9.4 97.3 %copy-start.52 = (f32[152]{0:T(256)}, f32[152]{0:T(256)S(1)}, u32[]{:S(2)}) copy-start(f32[152]{0:T(256)S(1)} %get-tuple-element.117) | copy-start | bytes 1828
  9.5 97.3 %copy-start.54 = (f32[152]{0:T(256)}, f32[152]{0:T(256)S(1)}, u32[]{:S(2)}) copy-start(f32[152]{0:T(256)S(1)} %get-tuple-element.118) | copy-start | bytes 1828
  10.8 95.9 %copy-start.56 = (f32[152]{0:T(256)}, f32[152]{0:T(256)S(1)}, u32[]{:S(2)}) copy-start(f32[152]{0:T(256)S(1)} %add_rsqrt_fusion.3) | copy-start | bytes 1828
  10.9 95.9 %copy-start.58 = (f32[152]{0:T(256)}, f32[152]{0:T(256)S(1)}, u32[]{:S(2)}) copy-start(f32[152]{0:T(256)S(1)} %add_rsqrt_fusion.1) | copy-start | bytes 1828
  33.2 73.6 %copy-start.50 = (f32[8,1,128]{2,1,0:T(1,128)}, f32[8,1,128]{2,1,0:T(1,128)S(1)}, u32[]{:S(2)}) copy-start(f32[8,1,128]{2,1,0:T(1,128)S(1)} %convert_element_type.589) | copy-start | bytes 12292
  51.8 157.3 %all-gather.17.cloned.1.call-start = ((), (), s32[]{:S(2)}) async-start(), calls=%async_computation.17 | async-start | bytes 1556480 | tf_op jit(solution)/shard_map/all_gather | solution.py:85
  52.6 230.2 %reduce-scatter.24.cloned.1.call-start = ((), (), s32[]{:S(2)}) async-start(), calls=%async_computation.18 | async-start | bytes 3112960 | tf_op jit(solution)/shard_map/reduce_scatter | solution.py:89
  73.4 143.2 %copy-start.92 = (f32[256]{0:T(256)}, f32[256]{0:T(256)S(1)}, u32[]{:S(2)}) copy-start(f32[256]{0:T(256)S(1)} %convert_element_type.595) | copy-start | bytes 3076
  106.8 346.6 %copy-start.8 = (bf16[1024,256]{1,0:T(8,128)(2,1)}, bf16[1024,256]{1,0:T(8,128)(2,1)S(1)}, u32[]{:S(2)}) copy-start(bf16[1024,256]{1,0:T(8,128)(2,1)S(1)} %all_gather.49) | copy-start | bytes 1572868
  171.9 37.3 %copy-start.12 = (bf16[1024,256]{1,0:T(8,128)(2,1)}, bf16[1024,256]{1,0:T(8,128)(2,1)S(1)}, u32[]{:S(2)}) copy-start(bf16[1024,256]{1,0:T(8,128)(2,1)S(1)} %all_gather.51) | copy-start | bytes 1572868
  228.6 37.2 %copy-start.83 = (bf16[128]{0:T(256)(128)(2,1)S(1)}, bf16[128]{0:T(256)(128)(2,1)}, u32[]{:S(2)}) copy-start(bf16[128]{0:T(256)(128)(2,1)} %param.31) | copy-start | bytes 772
  228.6 54.1 %copy-start.1 = (bf16[2,1,152,1024]{3,2,1,0:T(8,128)(2,1)S(1)}, bf16[2,1,152,1024]{3,2,1,0:T(8,128)(2,1)}, u32[]{:S(2)}) copy-start(bf16[2,1,152,1024]{3,2,1,0:T(8,128)(2,1)} %param.19) | copy-start | bytes 1867780
  230.7 54.6 %copy-start.24 = (bf16[2,1,152,1024]{3,2,1,0:T(8,128)(2,1)S(1)}, bf16[2,1,152,1024]{3,2,1,0:T(8,128)(2,1)}, u32[]{:S(2)}) copy-start(bf16[2,1,152,1024]{3,2,1,0:T(8,128)(2,1)} %param.37) | copy-start | bytes 1867780
  230.7 56.3 %copy-start.84 = (bf16[1,128]{1,0:T(2,128)(2,1)S(1)}, bf16[1,128]{1,0:T(2,128)(2,1)}, u32[]{:S(2)}) copy-start(bf16[1,128]{1,0:T(2,128)(2,1)} %param.33) | copy-start | bytes 772
  230.7 74.0 %all-gather.21.cloned.1.call-start = ((), (), s32[]{:S(2)}) async-start(), calls=%async_computation.20 | async-start | bytes 2359296 | tf_op jit(solution)/shard_map/all_gather | solution.py:34
  231.3 73.4 %all-gather.19.cloned.1.call-start = ((), (), s32[]{:S(2)}) async-start(), calls=%async_computation.19 | async-start | bytes 1556480 | tf_op jit(solution)/shard_map/all_gather | solution.py:85
  285.2 35.2 %all-gather.29.cloned.1.call-start = ((), (), s32[]{:S(2)}) async-start(), calls=%async_computation.27 | async-start | bytes 1556480 | tf_op jit(solution)/shard_map/all_gather | solution.py:93
  286.2 85.9 %all-gather.23.cloned.1.call-start = ((), (), s32[]{:S(2)}) async-start(), calls=%async_computation.21 | async-start | bytes 2359296 | tf_op jit(solution)/shard_map/all_gather | solution.py:35
  286.9 126.2 %reduce-scatter.32.cloned.1.call-start = ((), (), s32[]{:S(2)}) async-start(), calls=%async_computation.28 | async-start | bytes 3112960 | tf_op jit(solution)/shard_map/reduce_scatter | solution.py:97
  304.7 76.0 %copy-start.75 = (f32[1,1024]{1,0:T(1,128)}, f32[1,1024]{1,0:T(1,128)S(1)}, u32[]{:S(2)}) copy-start(f32[1,1024]{1,0:T(1,128)S(1)} %convert_element_type.586) | copy-start | bytes 12292
  380.6 68.8 %reduce-scatter.26.cloned.1.call-start = ((), (), s32[]{:S(2)}) async-start(), calls=%async_computation.22 | async-start | bytes 3112960 | tf_op jit(solution)/shard_map/reduce_scatter | solution.py:89
  386.0 84.9 %all-gather.31.cloned.1.call-start = ((), (), s32[]{:S(2)}) async-start(), calls=%async_computation.29 | async-start | bytes 1556480 | tf_op jit(solution)/shard_map/all_gather | solution.py:93
  404.6 48.5 %copy-start.72 = (f32[152]{0:T(256)}, f32[152]{0:T(256)S(1)}, u32[]{:S(2)}) copy-start(f32[152]{0:T(256)S(1)} %and_convert_fusion) | copy-start | bytes 1828
  415.1 38.3 %copy-start.6 = (bf16[1,608,1024]{2,1,0:T(8,128)(2,1)S(1)}, bf16[1,608,1024]{2,1,0:T(8,128)(2,1)}, u32[]{:S(2)}) copy-start(bf16[1,608,1024]{2,1,0:T(8,128)(2,1)} %all-gather.25.cloned.1.call-done) | copy-start | bytes 3735556
  415.1 38.3 %copy-start.93 = (f32[256]{0:T(256)S(1)}, f32[256]{0:T(256)}, u32[]{:S(2)}) copy-start(f32[256]{0:T(256)} %copy-done.92) | copy-start | bytes 3076
  453.1 72.9 %reduce-scatter.28.cloned.1.call-start = ((), (), s32[]{:S(2)}) async-start(), calls=%async_computation.24 | async-start | bytes 3112960 | tf_op jit(solution)/shard_map/reduce_scatter | solution.py:89
  492.0 54.1 %all-gather.27.cloned.1.call-start = ((), (), s32[]{:S(2)}) async-start(), calls=%async_computation.25 | async-start | bytes 1556480 | tf_op jit(solution)/shard_map/all_gather | solution.py:85
  528.3 36.9 %all-gather.33.cloned.1.call-start = ((), (), s32[]{:S(2)}) async-start(), calls=%async_computation.31 | async-start | bytes 1556480 | tf_op jit(solution)/shard_map/all_gather | solution.py:93
  528.9 78.3 %reduce-scatter.36.cloned.1.call-start = ((), (), s32[]{:S(2)}) async-start(), calls=%async_computation.32 | async-start | bytes 3112960 | tf_op jit(solution)/shard_map/reduce_scatter | solution.py:97
  573.2 70.7 %reduce-scatter.30.cloned.1.call-start = ((), (), s32[]{:S(2)}) async-start(), calls=%async_computation.26 | async-start | bytes 3112960 | tf_op jit(solution)/shard_map/reduce_scatter | solution.py:89
  578.6 65.3 %copy-start.25 = (bf16[2,1,152,1024]{3,2,1,0:T(8,128)(2,1)S(1)}, bf16[2,1,152,1024]{3,2,1,0:T(8,128)(2,1)}, u32[]{:S(2)}) copy-start(bf16[2,1,152,1024]{3,2,1,0:T(8,128)(2,1)} %param.37) | copy-start | bytes 1867780
  578.6 65.3 %copy-start.73 = (f32[152]{0:T(256)S(1)}, f32[152]{0:T(256)}, u32[]{:S(2)}) copy-start(f32[152]{0:T(256)} %copy-done.72) | copy-start | bytes 1828
  578.7 68.6 %copy-start.67 = (f32[4,608]{1,0:T(4,128)S(1)}, f32[4,608]{1,0:T(4,128)}, u32[]{:S(2)}) copy-start(f32[4,608]{1,0:T(4,128)} %get-tuple-element.48) | copy-start | bytes 29188
  578.7 68.6 %copy-start.71 = (f32[4,608]{1,0:T(4,128)S(1)}, f32[4,608]{1,0:T(4,128)}, u32[]{:S(2)}) copy-start(f32[4,608]{1,0:T(4,128)} %copy-done.70) | copy-start | bytes 29188
  578.7 68.6 %copy-start.44 = (bf16[608,256]{0,1:T(8,128)(2,1)S(1)}, bf16[608,256]{0,1:T(8,128)(2,1)}, u32[]{:S(2)}) copy-start(bf16[608,256]{0,1:T(8,128)(2,1)} %copy-done.43) | copy-start | bytes 933892
  578.7 86.3 %all-gather.35.cloned.1.call-start = ((), (), s32[]{:S(2)}) async-start(), calls=%async_computation.33 | async-start | bytes 1556480 | tf_op jit(solution)/shard_map/all_gather | solution.py:93
  647.2 122.5 %reduce-scatter.56.cloned.1.call-start = ((), (), s32[]{:S(2)}) async-start(), calls=%async_computation.43 | async-start | bytes 589824
  654.1 140.5 %reduce-scatter.54.cloned.1.call-start = ((), (), s32[]{:S(2)}) async-start(), calls=%async_computation.42 | async-start | bytes 147456
  693.1 165.2 %reduce-scatter.52.cloned.1.call-start = ((), (), s32[]{:S(2)}) async-start(), calls=%async_computation.41 | async-start | bytes 147456
  697.0 196.6 %reduce-scatter.38.cloned.1.call-start = ((), (), s32[]{:S(2)}) async-start(), calls=%async_computation.34 | async-start | bytes 3112960 | tf_op jit(solution)/shard_map/reduce_scatter | solution.py:97
  702.0 228.0 %reduce-scatter.34.cloned.1.call-start = ((), (), s32[]{:S(2)}) async-start(), calls=%async_computation.30 | async-start | bytes 3112960 | tf_op jit(solution)/shard_map/reduce_scatter | solution.py:97
  708.4 314.6 %reduce-scatter.50.cloned.1.call-start = ((), (), s32[]{:S(2)}) async-start(), calls=%async_computation.40 | async-start | bytes 4718592 | tf_op jit(solution)/shard_map/reduce_scatter | solution.py:448
  717.6 397.1 %reduce-scatter.48.cloned.1.call-start = ((), (), s32[]{:S(2)}) async-start(), calls=%async_computation.39 | async-start | bytes 4718592 | tf_op jit(solution)/shard_map/reduce_scatter | solution.py:447
  725.4 456.9 %reduce-scatter.46.cloned.1.call-start = ((), (), s32[]{:S(2)}) async-start(), calls=%async_computation.38 | async-start | bytes 1179648 | tf_op jit(solution)/shard_map/reduce_scatter | solution.py:446
  731.3 517.5 %reduce-scatter.44.cloned.1.call-start = ((), (), s32[]{:S(2)}) async-start(), calls=%async_computation.37 | async-start | bytes 1179648 | tf_op jit(solution)/shard_map/reduce_scatter | solution.py:445
  735.2 580.4 %reduce-scatter.40.cloned.1.call-start = ((), (), s32[]{:S(2)}) async-start(), calls=%async_computation.35 | async-start | bytes 1179648 | tf_op jit(solution)/shard_map/reduce_scatter | solution.py:443
  738.6 643.7 %reduce-scatter.42.cloned.1.call-start = ((), (), s32[]{:S(2)}) async-start(), calls=%async_computation.36 | async-start | bytes 1179648 | tf_op jit(solution)/shard_map/reduce_scatter | solution.py:444
  765.1 164.9 %copy-start.2 = (bf16[2,1,152,1024]{3,2,1,0:T(8,128)(2,1)S(1)}, bf16[2,1,152,1024]{3,2,1,0:T(8,128)(2,1)}, u32[]{:S(2)}) copy-start(bf16[2,1,152,1024]{3,2,1,0:T(8,128)(2,1)} %param.19) | copy-start | bytes 1867780
  765.1 164.9 %copy-start.51 = (f32[8,1,128]{2,1,0:T(1,128)S(1)}, f32[8,1,128]{2,1,0:T(1,128)}, u32[]{:S(2)}) copy-start(f32[8,1,128]{2,1,0:T(1,128)} %copy-done.50) | copy-start | bytes 12292
  765.1 164.9 %copy-start.53 = (f32[152]{0:T(256)S(1)}, f32[152]{0:T(256)}, u32[]{:S(2)}) copy-start(f32[152]{0:T(256)} %copy-done.52) | copy-start | bytes 1828
  765.1 164.9 %copy-start.55 = (f32[152]{0:T(256)S(1)}, f32[152]{0:T(256)}, u32[]{:S(2)}) copy-start(f32[152]{0:T(256)} %copy-done.54) | copy-start | bytes 1828
  765.1 164.9 %copy-start.57 = (f32[152]{0:T(256)S(1)}, f32[152]{0:T(256)}, u32[]{:S(2)}) copy-start(f32[152]{0:T(256)} %copy-done.56) | copy-start | bytes 1828
  765.1 164.9 %copy-start.59 = (f32[152]{0:T(256)S(1)}, f32[152]{0:T(256)}, u32[]{:S(2)}) copy-start(f32[152]{0:T(256)} %copy-done.58) | copy-start | bytes 1828
  766.8 210.6 %copy-start.26 = (f32[1,152,1024]{2,1,0:T(8,128)S(1)}, f32[1,152,1024]{2,1,0:T(8,128)}, u32[]{:S(2)}) copy-start(f32[1,152,1024]{2,1,0:T(8,128)} %get-tuple-element.76) | copy-start | bytes 1867780
  766.8 210.6 %copy-start.27 = (f32[1,152,1024]{2,1,0:T(8,128)S(1)}, f32[1,152,1024]{2,1,0:T(8,128)}, u32[]{:S(2)}) copy-start(f32[1,152,1024]{2,1,0:T(8,128)} %get-tuple-element.73) | copy-start | bytes 1867780
  (67 other events, 336.6 us)
Sparse Core Ops, SparseCore 0:
  51.9 16.5 all-gather.24
  70.0 17.8 all-gather.16
  230.8 31.1 reduce-scatter.23
  380.7 32.3 reduce-scatter.31
  415.5 33.8 reduce-scatter.25
  573.4 33.8 reduce-scatter.35
  610.0 33.8 reduce-scatter.29
Sparse Core Ops, SparseCore 1:
  233.5 46.5 all-gather.20
  285.3 15.8 all-gather.18
  302.6 17.6 all-gather.28
  322.7 49.3 all-gather.22
  453.2 17.7 all-gather.30
  492.1 33.7 reduce-scatter.27
  528.4 17.6 all-gather.26
  547.6 17.6 all-gather.32
  647.3 17.6 all-gather.34
  668.9 62.0 reduce-scatter.55
  734.5 59.9 reduce-scatter.53
  798.2 60.0 reduce-scatter.51
  860.8 32.8 reduce-scatter.37
  896.2 33.7 reduce-scatter.33
  934.7 88.2 reduce-scatter.49
  1027.2 87.5 reduce-scatter.47
  1119.1 63.2 reduce-scatter.45
  1186.3 62.5 reduce-scatter.43
  1253.1 62.5 reduce-scatter.39
  1319.6 62.6 reduce-scatter.41
where the time goes:
time: 1400 us; the launch traced here: 1390 us
  waiting for transfers between devices  821 us (59%)
  blocking collectives  341 us (24%)
  matrix products  145 us (10%)
  other arithmetic  38.5 us (3%)
  local copies, waits for them, and re-layouts  21.2 us (2%)
  between operations  21 us (2%)
    reduce_scatter x4, waiting for transfers between devices, collect_normed(): return lax.psum_scatter(partial_rows, 'mp', scatter_dimension=1, tiled=True)  108 us
    reduce_scatter x4, waiting for transfers between devices, collect_branch(): return lax.psum_scatter(partial_rows, 'mp', scatter_dimension=1, tiled=True)  103 us
    reduce_scatter x1, waiting for transfers between devices, on_device(): lax.psum_scatter(grad_up, 'dp', scatter_dimension=0, tiled=True)  91.7 us
    unnamed x30, waiting for transfers between devices  87.7 us
    reduce_scatter x1, waiting for transfers between devices, on_device(): lax.psum_scatter(grad_out, 'dp', scatter_dimension=0, tiled=True)  67.6 us
    reduce_scatter x1, waiting for transfers between devices, on_device(): lax.psum_scatter(grad_query, 'dp', scatter_dimension=0, tiled=True)  66.7 us
    reduce_scatter x1, waiting for transfers between devices, on_device(): lax.psum_scatter(grad_key, 'dp', scatter_dimension=0, tiled=True)  66.7 us
    reduce_scatter x1, waiting for transfers between devices, on_device(): lax.psum_scatter(grad_value, 'dp', scatter_dimension=0, tiled=True)  66.5 us
  transfers between devices with their start and end apart: 27, of which 21 were waited for; matrix products, arithmetic and copies ran while one was open for 9% of the time, Pallas kernels for 0%

commit v1 on v0

v1 whole, which is shorter than its diff:
```python
import functools
import math

import jax
import jax.numpy as jnp
from jax import lax
from jax.experimental import pallas as pl
from jax.experimental.pallas import tpu as pltpu
from jax.sharding import PartitionSpec as P

HD = 64
IMG_LEN = 577
F32 = jnp.float32
BF16 = jnp.bfloat16
MESH = pl.DeviceIdType.MESH
TILE = 256
PQ, PK, PV, PO = 0, 1, 2, 3
G1, S1, OB, G2, S2, DB, UB, QB, VB = 0, 1, 2, 3, 4, 5, 6, 8, 9
DG1, DS1, DOB, DG2, DS2, DDB, DUB, DQB, DVB, PEAK = 0, 1, 2, 3, 4, 5, 6, 7, 8, 9


def dot_nn(left, right):
    return lax.dot_general(left, right, (((1,), (0,)), ((), ())), preferred_element_type=F32)


def dot_nt(left, right):
    return lax.dot_general(left, right, (((1,), (1,)), ((), ())), preferred_element_type=F32)


def dot_tn(left, right):
    return lax.dot_general(left, right, (((0,), (0,)), ((), ())), preferred_element_type=F32)


def standardize(rows):
    center = rows - jnp.mean(rows, axis=-1, keepdims=True)
    inverse = lax.rsqrt(jnp.mean(center * center, axis=-1, keepdims=True) + 1e-05)
    return center * inverse, inverse


def norm_back(incoming, scaled, inverse, gain):
    upward = incoming * gain
    return inverse * (
        upward
        - jnp.mean(upward, axis=-1, keepdims=True)
        - scaled * jnp.mean(upward * scaled, axis=-1, keepdims=True)
    )


def each(low, high, body):
    if high - low <= 8:
        for at in range(low, high):
            body(at)
    else:

        def step(at, carry):
            body(at)
            return carry

        lax.fori_loop(low, high, step, 0)


def sum_rows(rows):
    return jnp.sum(rows, axis=0, keepdims=True)


class Layer:
    def __init__(self, size, refs):
        self.__dict__.update(size)
        self.__dict__.update(refs)
        self.dp_at = lax.axis_index("dp")
        self.mp_at = lax.axis_index("mp")
        self.line_at = self.dp_at // 2
        self.pair_at = lax.rem(self.dp_at, 2)
        self.chip_at = self.mp_at // 2
        self.core_at = lax.rem(self.mp_at, 2)
        self.sib = (self.dp_at, self.chip_at * 2 + 1 - self.core_at)
        self.across = (self.dp_at, (1 - self.chip_at) * 2 + self.core_at)
        self.pair = (self.line_at * 2 + 1 - self.pair_at, self.mp_at)
        self.stage_sends = [[], []]
        self.spread_sends = [[], [], [], []]
        self.late = []

    def line_of(self, step):
        return lax.rem(self.line_at + step + self.lines, self.lines)

    def line_peer(self, step):
        return (self.line_of(step) * 2 + self.pair_at, self.mp_at)

    def slot(self, line, pair):
        return pl.ds(pl.multiple_of((line * 2 + pair) * self.shard, self.shard), self.shard)

    def block(self, micro, chip, core):
        start = micro * self.rows + (chip * 2 + core) * self.pad
        return pl.ds(pl.multiple_of(start, 16), self.pad)

    def own_block(self, micro):
        return self.block(micro, self.chip_at, self.core_at)

    def source(self, piece):
        if piece < 4:
            return (self.query_w, self.key_w, self.value_w, self.out_w)[piece]
        which, chunk = (piece - 4) % 2, (piece - 4) // 2
        return (self.up_w, self.down_w)[which].at[:, pl.ds(chunk * TILE, TILE)]

    def copy(self, src, dst, send_sem, recv_sem, device):
        return pltpu.make_async_remote_copy(
            src_ref=src,
            dst_ref=dst,
            send_sem=send_sem,
            recv_sem=recv_sem,
            device_id=device,
            device_id_type=MESH,
        )

    def weight_line(self, piece, step):
        return self.copy(
            self.source(piece),
            self.weights.at[piece, self.slot(self.line_at, self.pair_at)],
            self.wz_send.at[piece, step - 1],
            self.wz_recv.at[piece, step - 1],
            self.line_peer(step),
        )

    def weight_line_in(self, piece, step):
        place = self.weights.at[piece, self.slot(self.line_of(-step), self.pair_at)]
        return self.copy(
            place,
            place,
            self.wz_send.at[piece, step - 1],
            self.wz_recv.at[piece, step - 1],
            self.line_peer(-step),
        )

    def weight_pair(self, piece, step, own):
        place = self.weights.at[piece, self.slot(self.line_of(-step), self.pair_at)]
        return self.copy(
            self.source(piece) if own else place,
            place,
            self.wx_send.at[piece, step],
            self.wx_recv.at[piece, step],
            self.pair,
        )

    def weight_pair_in(self, piece, step):
        place = self.weights.at[piece, self.slot(self.line_of(-step), 1 - self.pair_at)]
        return self.copy(
            place, place, self.wx_send.at[piece, step], self.wx_recv.at[piece, step], self.pair
        )

    def weight_local(self, piece):
        return pltpu.make_async_copy(
            self.source(piece),
            self.weights.at[piece, self.slot(self.line_at, self.pair_at)],
            self.wl_sem.at[piece],
        )

    def send_weight(self, piece):
        self.weight_pair(piece, 0, True).start()
        each(1, self.lines, lambda step: self.weight_line(piece, step).start())
        self.weight_local(piece).start()

    def pass_weight(self, piece):
        def one(step):
            self.weight_line_in(piece, step).wait_recv()
            self.weight_pair(piece, step, False).start()

        each(1, self.lines, one)

    def await_weight(self, piece):
        self.weight_local(piece).wait()
        each(0, self.lines, lambda step: self.weight_pair_in(piece, step).wait_recv())

    def spread_copy(self, kind, micro, ref, which):
        place = ref.at[self.own_block(micro)]
        if which == 2:
            place = ref.at[self.block(micro, 1 - self.chip_at, self.core_at)]
        return self.copy(
            place,
            place,
            self.ag_send.at[kind, micro, which],
            self.ag_recv.at[kind, micro, which],
            self.across if which == 0 else self.sib,
        )

    def spread_in(self, kind, micro, ref, which):
        chip = self.chip_at if which == 1 else 1 - self.chip_at
        core = self.core_at if which == 0 else 1 - self.core_at
        place = ref.at[self.block(micro, chip, core)]
        return self.copy(
            place,
            place,
            self.ag_send.at[kind, micro, which],
            self.ag_recv.at[kind, micro, which],
            self.across if which == 0 else self.sib,
        )

    def spread(self, kind, micro, ref):
        for which in (0, 1):
            one = self.spread_copy(kind, micro, ref, which)
            one.start()
            self.spread_sends[kind].append(one)

    def spread_on(self, kind, micro, ref):
        self.spread_in(kind, micro, ref, 0).wait_recv()
        one = self.spread_copy(kind, micro, ref, 2)
        one.start()
        self.spread_sends[kind].append(one)

    def spread_sent(self, kind):
        for one in self.spread_sends[kind]:
            one.wait_send()
        self.spread_sends[kind] = []

    def spread_end(self, kind, micro, ref):
        self.spread_in(kind, micro, ref, 1).wait_recv()
        self.spread_in(kind, micro, ref, 2).wait_recv()

    def collect(self, kind, micro, terms):
        for one in self.stage_sends[micro]:
            one.wait_send()
        self.stage_sends[micro] = []
        stage, keep = self.stage, self.keep_own.at[1 if kind == 1 else 0, micro]

        def fill(ref, at, chip, core):
            def step(tile, carry):
                cols = pl.ds(pl.multiple_of(tile * TILE, TILE), TILE)
                product = terms(self.block(micro, chip, core), cols)
                ref[at + (slice(None), cols)] = product.astype(ref.dtype)
                return carry

            lax.fori_loop(0, self.width // TILE, step, 0)

        for half in (0, 1):
            chip = 1 - self.chip_at if half == 0 else self.chip_at
            fill(stage, (micro, half), chip, 1 - self.core_at)
            one = self.copy(
                stage.at[micro, half],
                self.sib_in.at[kind, micro, half],
                self.rs_send.at[kind, micro, half],
                self.rs_recv.at[kind, micro, half],
                self.sib,
            )
            one.start()
            self.stage_sends[micro].append(one)
            if half == 0:
                fill(self.keep_far, (), chip, self.core_at)
        incoming = self.sib_in.at[kind, micro, 0]
        self.copy(
            stage.at[micro, 0],
            incoming,
            self.rs_send.at[kind, micro, 0],
            self.rs_recv.at[kind, micro, 0],
            self.sib,
        ).wait_recv()
        incoming[...] = (self.keep_far[...] + incoming[...].astype(F32)).astype(BF16)
        one = self.copy(
            incoming,
            self.far_in.at[kind, micro],
            self.rs_send.at[kind, micro, 2],
            self.rs_recv.at[kind, micro, 2],
            self.across,
        )
        one.start()
        self.late.append(one)
        fill(keep, (), self.chip_at, self.core_at)

    def collected(self, kind, micro):
        near, far = self.sib_in.at[kind, micro, 1], self.far_in.at[kind, micro]
        self.copy(
            near, near, self.rs_send.at[kind, micro, 1], self.rs_recv.at[kind, micro, 1], self.sib
        ).wait_recv()
        self.copy(
            far, far, self.rs_send.at[kind, micro, 2], self.rs_recv.at[kind, micro, 2], self.across
        ).wait_recv()
        total = self.keep_own[1 if kind == 1 else 0, micro] + near[...].astype(F32)
        return (total + far[...].astype(F32))[: self.part]

    def summed(self, piece):
        return self.weights.at[piece] if piece < 4 else self.wide_sums.at[piece - 4]

    def grad_pair(self, piece, line):
        return self.copy(
            self.summed(piece).at[self.slot(line, 1 - self.pair_at)],
            self.pair_in.at[piece, line],
            self.gx_send.at[piece, line],
            self.gx_recv.at[piece, line],
            self.pair,
        )

    def grad_line(self, piece, step):
        return self.copy(
            self.pair_in.at[piece, self.line_of(step)],
            self.line_in.at[piece, step - 1],
            self.gz_send.at[piece, step - 1],
            self.gz_recv.at[piece, step - 1],
            self.line_peer(step),
        )

    def grad_start(self, piece, left, right):
        out = self.summed(piece)
        lines_in_tile = TILE // (2 * self.shard)

        def step(tile, carry):
            cols = pl.ds(pl.multiple_of(tile * TILE, TILE), TILE)
            out[cols, :] = dot_tn(left[:, cols], right).astype(BF16)
            for at in range(lines_in_tile):
                self.grad_pair(piece, tile * lines_in_tile + at).start()
            return carry

        lax.fori_loop(0, self.width // TILE, step, 0)

    def grad_pass(self, piece):
        def one(step):
            line = self.line_of(step)
            self.grad_pair(piece, line).wait_recv()
            mine = self.summed(piece)[self.slot(line, self.pair_at), :].astype(F32)
            mine = mine + self.pair_in[piece, line].astype(F32)
            self.pair_in[piece, line] = mine.astype(BF16)
            self.grad_line(piece, step).start()

        each(1, self.lines, one)

    def grad_end(self, piece):
        self.grad_pair(piece, self.line_at).wait_recv()
        total = self.summed(piece)[self.slot(self.line_at, self.pair_at), :].astype(F32)
        total = total + self.pair_in[piece, self.line_at].astype(F32)
        for step in range(1, self.lines):
            self.grad_line(piece, step).wait_recv()
            total = total + self.line_in[piece, step - 1].astype(F32)
        if piece < 4:
            (self.query_g, self.key_g, self.value_g, self.out_g)[piece][...] = total
        else:
            which, chunk = (piece - 4) % 2, (piece - 4) // 2
            (self.up_g, self.down_g)[which][:, chunk * TILE : (chunk + 1) * TILE] = total

    def vector_copy(self, step):
        return self.copy(
            self.packed,
            self.vectors_in.at[self.dp_at],
            self.v_send.at[0, step - 1],
            self.v_recv.at[0, step - 1],
            (lax.rem(self.dp_at + step, self.dps), self.mp_at),
        )

    def vector_copy_in(self, step):
        origin = lax.rem(self.dp_at - step + self.dps, self.dps)
        place = self.vectors_in.at[origin]
        return self.copy(
            place,
            place,
            self.v_send.at[0, step - 1],
            self.v_recv.at[0, step - 1],
            (origin, self.mp_at),
        )

    def share_copy(self, step):
        target = lax.rem(self.dp_at + step, self.dps)
        return self.copy(
            self.shares.at[target],
            self.shares_in.at[step - 1],
            self.v_send.at[1, step - 1],
            self.v_recv.at[1, step - 1],
            (target, self.mp_at),
        )

    def group_copy(self, step):
        return self.copy(
            self.group.at[0],
            self.group.at[step],
            self.m_send.at[step - 1],
            self.m_recv.at[step - 1],
            (self.dp_at, lax.rem(self.mp_at + step, 4)),
        )

    def take_vectors(self):
        if not self.own_vectors:
            self.vectors[...] = self.packed[...]
            return
        self.vectors_in[self.dp_at] = self.packed[...]
        for step in range(1, self.dps):
            self.vector_copy_in(step).wait_recv()
        rest = self.vectors_in[0, 8:16, :]
        for at in range(1, self.dps):
            rest = rest + self.vectors_in[at, 8:16, :]
        for at in range(self.dps):
            self.vectors[0:8, at * 128 : (at + 1) * 128] = self.vectors_in[at, 0:8, :]
        for row, first in ((QB, 0), (VB, 2)):
            self.vectors[row : row + 1, 0:128] = rest[first : first + 1]
            self.vectors[row : row + 1, 128:256] = rest[first + 1 : first + 2]

    def give_vectors(self):
        if not self.own_vectors:
            self.vector_g[...] = self.sums[...]
            return
        for at in range(self.dps):
            half = (at * 32 // 128) * 128
            self.shares[at, 0:7, :] = self.sums[0:7, at * 128 : (at + 1) * 128]
            self.shares[at, 7:9, :] = self.sums[7:9, half : half + 128]
            self.shares[at, 9:16, :] = self.sums[9:16, 0:128]
        for step in range(1, self.dps):
            self.share_copy(step).start()

    def end_vectors(self):
        if not self.own_vectors:
            return
        total = self.shares[self.dp_at]
        most = total[PEAK : PEAK + 1]
        for step in range(1, self.dps):
            self.share_copy(step).wait_recv()
            came = self.shares_in[step - 1]
            total = total + came
            most = jnp.maximum(most, came[PEAK : PEAK + 1])
        self.group[0] = total
        for step in range(1, 4):
            self.group_copy(step).start()
        whole = total[0:6]
        for step in range(1, 4):
            self.group_copy(step).wait_recv()
            whole = whole + self.group[step, 0:6, :]
        self.vector_g[0:6, :] = whole
        self.vector_g[6:9, :] = total[6:9]
        self.vector_g[9:10, :] = most
        self.vector_g[10:16, :] = jnp.zeros((6, 128), F32)

    def vector(self, row, start=0, size=None):
        size = self.width if size is None else size
        return self.vectors[row : row + 1, pl.ds(start, size)]

    def add_sum(self, row, value, start=0):
        cols = pl.ds(start, value.shape[1])
        self.sums[row : row + 1, cols] = self.sums[row : row + 1, cols] + value

    def mask(self, micro):
        row = self.mp_at * self.part + lax.broadcasted_iota(jnp.int32, (self.part, 1), 0)
        live = jnp.where(self.counts[micro, 0] > 0, 1.0, 0.0).astype(F32)
        return jnp.where(row < IMG_LEN, live, 0.0)

    def put_rows(self, ref, micro, rows):
        filler = jnp.zeros((self.pad - self.part, self.width), F32)
        ref[self.own_block(micro), :] = jnp.concatenate([rows, filler], axis=0).astype(BF16)

    def first_norm(self, micro):
        scaled, _ = standardize(self.images[micro, 0].astype(F32))
        self.put_rows(self.normed_one, micro, scaled * self.vector(G1) + self.vector(S1))
        self.spread(0, micro, self.normed_one)

    def out_rows(self, micro):
        return self.out_grad[micro, 0].astype(F32) * self.mask(micro)

    def project_back(self, micro):
        rows = self.out_rows(micro)
        self.put_rows(self.proj_back, micro, rows)
        self.add_sum(DDB, sum_rows(rows.astype(BF16).astype(F32)))
        self.spread(2, micro, self.proj_back)

    def second_norm(self, micro):
        rows = self.images[micro, 0].astype(F32) + self.collected(0, micro) + self.vector(OB)
        self.after_attn[micro] = rows
        scaled, _ = standardize(rows)
        self.put_rows(self.normed_two, micro, scaled * self.vector(G2) + self.vector(S2))
        self.spread(1, micro, self.normed_two)

    def give_result(self, micro):
        rows = self.after_attn[micro] + self.collected(1, micro) + self.vector(DB)
        self.result[micro, 0] = (self.mask(micro) * rows).astype(BF16)

    def second_norm_back(self, micro):
        incoming = self.collected(2, micro)
        scaled, inverse = standardize(self.after_attn[micro])
        rows = self.out_rows(micro) + norm_back(incoming, scaled, inverse, self.vector(G2))
        self.attn_back[micro] = rows
        self.add_sum(DOB, sum_rows(rows.astype(BF16).astype(F32)))
        self.add_sum(DG2, sum_rows(incoming * scaled))
        self.add_sum(DS2, sum_rows(incoming))
        self.put_rows(self.attended_back, micro, rows)
        self.spread(3, micro, self.attended_back)

    def first_norm_back(self, micro):
        incoming = self.collected(3, micro)
        scaled, inverse = standardize(self.images[micro, 0].astype(F32))
        self.add_sum(DG1, sum_rows(incoming * scaled))
        self.add_sum(DS1, sum_rows(incoming))
        rows = self.attn_back[micro] + norm_back(incoming, scaled, inverse, self.vector(G1))
        self.input_grad[micro, 0] = rows.astype(BF16)

    def image_rows(self, micro):
        return pl.ds(micro * self.rows, self.rows)

    def counted(self, axis):
        shape = (self.rows, 1) if axis == 0 else (1, self.rows)
        row = lax.broadcasted_iota(jnp.int32, shape, axis)
        block = row // self.pad
        inside = row - block * self.pad
        return (inside < self.part) & (block * self.part + inside < IMG_LEN)

    def head_columns(self, head):
        column = lax.broadcasted_iota(jnp.int32, (self.rows, TILE), 1)
        return column // HD == head

    def project_heads(self, micro):
        rows = self.image_rows(micro)
        normed = self.normed_one[rows, :]
        scale = 1.0 / math.sqrt(HD)
        query = dot_nn(normed, self.weights[PQ]) + self.vector(QB, 0, TILE)
        self.queries[rows, :] = (query.astype(BF16).astype(F32) * scale).astype(BF16)
        self.keys[rows, :] = dot_nn(normed, self.weights[PK]).astype(BF16)
        value = dot_nn(normed, self.weights[PV]) + self.vector(VB, 0, TILE)
        self.values[rows, :] = value.astype(BF16)

    def attend(self, micro):
        rows = self.image_rows(micro)
        self.turned[...] = self.values[rows, :].T
        live = jnp.where(self.counts[micro, 0] > 0, 0.0, -1e30).astype(F32)

        def one_head(head, carry):
            query = jnp.where(self.head_columns(head), self.queries[rows, :], jnp.zeros((), BF16))
            scores = dot_nt(self.keys[rows, :], query)
            scores = jnp.where(self.counted(0), scores, -1e30)
            top = jnp.max(scores, axis=0, keepdims=True)
            expo = jnp.exp(scores - top)
            total = jnp.sum(expo, axis=0, keepdims=True)
            self.log_total[micro, head] = top + jnp.log(total)
            cols = pl.ds(pl.multiple_of(head * HD, HD), HD)
            mixed = dot_nn(self.turned[cols, :], expo.astype(BF16))
            self.mixed_turned[micro, cols, :] = mixed * (1.0 / total)
            peak = jnp.max(jnp.where(self.counted(1), top, -1e30), axis=1, keepdims=True)
            peak = jnp.where(live < 0.0, -1e30, peak)
            lane = lax.broadcasted_iota(jnp.int32, (1, 128), 1)
            seen = self.sums[PEAK : PEAK + 1, 0:128]
            self.sums[PEAK : PEAK + 1, 0:128] = jnp.where(
                lane == head, jnp.maximum(seen, peak), seen
            )
            return carry

        lax.fori_loop(0, self.heads, one_head, 0)
        self.mixed[rows, :] = self.mixed_turned[micro].T.astype(BF16)

    def attend_back(self, micro):
        rows = self.image_rows(micro)
        self.mixed_back[...] = dot_nn(self.attended_back[rows, :], self.weights[PO]).astype(BF16)
        self.turned[...] = self.keys[rows, :].T
        self.mixed_back_turned[...] = self.mixed_back[...].T
        self.key_sum[...] = jnp.zeros_like(self.key_sum)
        self.value_sum[...] = jnp.zeros_like(self.value_sum)
        chunk = self.rows // 2

        def one_head(head, carry):
            columns = self.head_columns(head)
            none = jnp.zeros((), BF16)
            query = jnp.where(columns, self.queries[rows, :], none)
            outward = jnp.where(columns, self.mixed_back[...], none)
            cols = pl.ds(pl.multiple_of(head * HD, HD), HD)
            dots = self.mixed_back_turned[cols, :].astype(F32) * self.mixed_turned[micro, cols, :]
            delta = jnp.sum(dots, axis=0, keepdims=True)
            log_total = self.log_total[micro, head]
            for at in range(2):
                part = pl.ds(micro * self.rows + at * chunk, chunk)
                here = pl.ds(at * chunk, chunk)
                scores = dot_nt(self.keys[part, :], query)
                counted = self.counted(0)[at * chunk : (at + 1) * chunk]
                probs = jnp.where(counted, jnp.exp(scores - log_total), 0.0)
                prob_back = dot_nt(self.values[part, :], outward)
                self.probs[here, :] = probs.astype(BF16)
                self.score_back[here, :] = (probs * (prob_back - delta)).astype(BF16)
            self.value_sum[...] += dot_nn(self.probs[...], outward)
            self.key_sum[...] += dot_nn(self.score_back[...], query)
            self.query_turned[cols, :] = dot_nn(self.turned[cols, :], self.score_back[...])
            return carry

        lax.fori_loop(0, self.heads, one_head, 0)
        scale = 1.0 / math.sqrt(HD)
        query_back = (self.query_turned[...] * scale).T.astype(BF16)
        value_back = self.value_sum[...].astype(BF16)
        self.queries[rows, :] = query_back
        self.keys[rows, :] = self.key_sum[...].astype(BF16)
        self.values[rows, :] = value_back
        self.add_sum(DQB, sum_rows(query_back.astype(F32)))
        self.add_sum(DVB, sum_rows(value_back.astype(F32)))

    def feed(self, micro, chunk):
        cols = pl.ds(chunk * TILE, TILE)
        up, down = self.weights.at[4 + 2 * chunk], self.weights.at[5 + 2 * chunk]
        part = self.rows // 2
        total = jnp.zeros((1, TILE), F32)
        for at in range(2):
            rows = pl.ds(micro * self.rows + at * part, part)
            hidden = dot_nn(self.normed_two[rows, :], up[...])
            hidden = hidden + self.vector(UB, chunk * TILE, TILE)
            gate = jax.nn.sigmoid(1.702 * hidden)
            self.activated[rows, cols] = (hidden * gate).astype(BF16)
            back = dot_nn(self.proj_back[rows, :], down[...])
            back = back * (gate + 1.702 * hidden * gate * (1.0 - gate))
            back = back.astype(BF16)
            self.pre_back[rows, cols] = back
            total = total + sum_rows(back.astype(F32))
        self.add_sum(DUB, total, chunk * TILE)

    def out_terms(self, rows, cols):
        return dot_nt(self.mixed[rows, :], self.weights[PO, cols, :])

    def wide_terms(self, ref, first):
        def terms(rows, cols):
            total = None
            for chunk in range(self.chunks):
                one = dot_nt(
                    ref[rows, chunk * TILE : (chunk + 1) * TILE],
                    self.weights[first + 2 * chunk, cols, :],
                )
                total = one if total is None else total + one
            return total

        return terms

    def input_terms(self, rows, cols):
        total = dot_nt(self.queries[rows, :], self.weights[PQ, cols, :])
        total = total + dot_nt(self.keys[rows, :], self.weights[PK, cols, :])
        return total + dot_nt(self.values[rows, :], self.weights[PV, cols, :])

    def enter(self):
        barrier = pltpu.get_barrier_semaphore()
        peers = [self.sib, self.across]
        if self.own_vectors:
            peers.append((self.dp_at, (1 - self.chip_at) * 2 + 1 - self.core_at))
        for peer in peers:
            pl.semaphore_signal(barrier, inc=1, device_id=peer, device_id_type=MESH)
        if self.own_vectors:

            def hail(step):
                peer = (lax.rem(self.dp_at + step, self.dps), self.mp_at)
                pl.semaphore_signal(barrier, inc=1, device_id=peer, device_id_type=MESH)

            each(1, self.dps, hail)
            pl.semaphore_wait(barrier, 3 + self.dps - 1)
        else:
            pl.semaphore_signal(barrier, inc=1, device_id=self.pair, device_id_type=MESH)

            def hail(step):
                peer = self.line_peer(step)
                pl.semaphore_signal(barrier, inc=1, device_id=peer, device_id_type=MESH)

            each(1, self.lines, hail)
            pl.semaphore_wait(barrier, 2 + self.lines)

    def run(self):
        pieces = 4 + 2 * self.chunks
        self.enter()
        if self.own_vectors:
            for step in range(1, self.dps):
                self.vector_copy(step).start()
        for piece in range(4):
            self.send_weight(piece)
        self.sums[...] = jnp.zeros_like(self.sums)
        self.sums[PEAK : PEAK + 1, :] = jnp.full((1, self.width), -1e30, F32)
        self.take_vectors()
        for micro in (0, 1):
            self.first_norm(micro)
        for micro in (0, 1):
            self.project_back(micro)
        for piece in range(3):
            self.pass_weight(piece)
        for piece in range(4, pieces):
            self.send_weight(piece)
        for micro in (0, 1):
            self.spread_on(0, micro, self.normed_one)
        self.pass_weight(3)
        for piece in range(3):
            self.await_weight(piece)
        waiting = list(range(4, pieces))
        for micro in (0, 1):
            self.spread_end(0, micro, self.normed_one)
            self.project_heads(micro)
            self.attend(micro)
            if micro == 0:
                self.await_weight(PO)
            else:
                self.second_norm(0)
            self.collect(0, micro, self.out_terms)
            self.spread_on(2, micro, self.proj_back)
            self.pass_weight(waiting.pop(0))
        self.spread_on(1, 0, self.normed_two)
        self.second_norm(1)
        self.pass_weight(waiting.pop(0))
        self.pass_weight(waiting.pop(0))
        self.spread_on(1, 1, self.normed_two)
        for micro in (0, 1):
            self.spread_end(1, micro, self.normed_two)
            self.spread_end(2, micro, self.proj_back)
        for chunk in range(self.chunks):
            up, down = 4 + 2 * chunk, 5 + 2 * chunk
            self.await_weight(up)
            self.await_weight(down)
            for micro in (0, 1):
                self.feed(micro, chunk)
            cols = slice(chunk * TILE, (chunk + 1) * TILE)
            self.grad_start(up, self.normed_two, self.pre_back[:, cols])
            self.grad_start(down, self.proj_back, self.activated[:, cols])
            for _ in range(2):
                if waiting:
                    self.pass_weight(waiting.pop(0))
            if chunk:
                self.grad_pass(up - 2)
                self.grad_pass(down - 2)
        self.spread_sent(1)
        for micro in (0, 1):
            self.collect(2, micro, self.wide_terms(self.pre_back, 4))
        self.grad_pass(pieces - 2)
        self.grad_pass(pieces - 1)
        for micro in (0, 1):
            self.collect(1, micro, self.wide_terms(self.activated, 5))
            self.second_norm_back(micro)
        for micro in (0, 1):
            self.spread_on(3, micro, self.attended_back)
            self.spread_end(3, micro, self.attended_back)
            self.attend_back(micro)
            self.collect(3, micro, self.input_terms)
        for piece in range(4):
            each(1, self.lines, lambda step: self.weight_pair(piece, step, False).wait_send())
        self.grad_start(PO, self.attended_back, self.mixed[...])
        self.grad_start(PQ, self.normed_one, self.queries[...])
        self.grad_start(PK, self.normed_one, self.keys[...])
        self.grad_start(PV, self.normed_one, self.values[...])
        for micro in (0, 1):
            self.first_norm_back(micro)
        self.give_vectors()
        for piece in (PO, PQ, PK, PV):
            self.grad_pass(piece)
        for micro in (0, 1):
            self.give_result(micro)
        for piece in range(4, pieces):
            self.grad_end(piece)
        self.end_vectors()
        for piece in (PO, PQ, PK, PV):
            self.grad_end(piece)
        for kind in (0, 2, 3):
            self.spread_sent(kind)
        for one in self.late + self.stage_sends[0] + self.stage_sends[1]:
            one.wait_send()
        for piece in range(pieces):
            self.weight_pair(piece, 0, True).wait_send()
            each(1, self.lines, lambda step: self.weight_line(piece, step).wait_send())
            if piece >= 4:
                each(1, self.lines, lambda step: self.weight_pair(piece, step, False).wait_send())
            each(0, self.lines, lambda line: self.grad_pair(piece, line).wait_send())
            each(1, self.lines, lambda step: self.grad_line(piece, step).wait_send())
        if self.own_vectors:
            for step in range(1, self.dps):
                self.vector_copy(step).wait_send()
                self.share_copy(step).wait_send()
            for step in range(1, 4):
                self.group_copy(step).wait_send()


def layer_kernel(size, names, *refs):
    named = dict(zip(names, refs))
    named["attended_back"] = named["normed_two"]
    Layer(size, named).run()


def fused_layer(size, counts, images, out_grad, packed, weights):
    width, shard, part, rows, pad = (size[key] for key in ("width", "shard", "part", "rows", "pad"))
    lines, dps, pieces = size["lines"], size["dps"], 4 + 2 * size["chunks"]
    units = size["chunks"] * TILE
    vmem = pl.BlockSpec(memory_space=pltpu.VMEM)
    anywhere = pl.BlockSpec(memory_space=pl.ANY)
    vector_shape = (16, 128) if size["own_vectors"] else (16, width)
    outputs = {
        "result": (images.shape, BF16),
        "input_grad": (images.shape, BF16),
        "query_g": ((shard, TILE), F32),
        "key_g": ((shard, TILE), F32),
        "value_g": ((shard, TILE), F32),
        "out_g": ((shard, TILE), F32),
        "up_g": ((shard, units), F32),
        "down_g": ((shard, units), F32),
        "vector_g": (vector_shape, F32),
    }
    dma = pltpu.SemaphoreType.DMA
    vm = pltpu.VMEM
    scratch = {
        "weights": vm((pieces, width, TILE), BF16),
        "normed_one": vm((2 * rows, width), BF16),
        "normed_two": vm((2 * rows, width), BF16),
        "proj_back": vm((2 * rows, width), BF16),
        "queries": vm((2 * rows, TILE), BF16),
        "keys": vm((2 * rows, TILE), BF16),
        "values": vm((2 * rows, TILE), BF16),
        "mixed": vm((2 * rows, TILE), BF16),
        "mixed_turned": vm((2, TILE, rows), F32),
        "log_total": vm((2, size["heads"], 1, rows), F32),
        "activated": vm((2 * rows, units), BF16),
        "pre_back": vm((2 * rows, units), BF16),
        "turned": vm((TILE, rows), BF16),
        "mixed_back": vm((rows, TILE), BF16),
        "mixed_back_turned": vm((TILE, rows), BF16),
        "query_turned": vm((TILE, rows), F32),
        "key_sum": vm((rows, TILE), F32),
        "value_sum": vm((rows, TILE), F32),
        "probs": vm((rows, rows), BF16),
        "score_back": vm((rows, rows), BF16),
        "stage": vm((2, 2, pad, width), BF16),
        "keep_far": vm((pad, width), F32),
        "keep_own": vm((2, 2, pad, width), F32),
        "sib_in": vm((4, 2, 2, pad, width), BF16),
        "far_in": vm((4, 2, pad, width), BF16),
        "after_attn": vm((2, part, width), F32),
        "attn_back": vm((2, part, width), F32),
        "wide_sums": vm((pieces - 4, width, TILE), BF16),
        "pair_in": vm((pieces, lines, shard, TILE), BF16),
        "line_in": vm((pieces, lines - 1, shard, TILE), BF16),
        "vectors": vm((16, width), F32),
        "sums": vm((16, width), F32),
        "wz_send": dma((pieces, lines - 1)),
        "wz_recv": dma((pieces, lines - 1)),
        "wx_send": dma((pieces, lines)),
        "wx_recv": dma((pieces, lines)),
        "wl_sem": dma((pieces,)),
        "ag_send": dma((4, 2, 3)),
        "ag_recv": dma((4, 2, 3)),
        "rs_send": dma((4, 2, 3)),
        "rs_recv": dma((4, 2, 3)),
        "gx_send": dma((pieces, lines)),
        "gx_recv": dma((pieces, lines)),
        "gz_send": dma((pieces, lines - 1)),
        "gz_recv": dma((pieces, lines - 1)),
    }
    if size["own_vectors"]:
        scratch |= {
            "vectors_in": vm((dps, 16, 128), F32),
            "shares": vm((dps, 16, 128), F32),
            "shares_in": vm((dps - 1, 16, 128), F32),
            "group": vm((4, 16, 128), F32),
            "v_send": dma((2, dps - 1)),
            "v_recv": dma((2, dps - 1)),
            "m_send": dma((3,)),
            "m_recv": dma((3,)),
        }
    inputs = ["counts", "images", "out_grad", "packed"]
    inputs += ["query_w", "key_w", "value_w", "out_w", "up_w", "down_w"]
    names = inputs + list(outputs) + list(scratch)
    return pl.pallas_call(
        functools.partial(layer_kernel, size, names),
        out_shape=[jax.ShapeDtypeStruct(*spec) for spec in outputs.values()],
        in_specs=[pl.BlockSpec(memory_space=pltpu.SMEM)] + [vmem] * 3 + [anywhere] * 6,
        out_specs=[vmem] * len(outputs),
        scratch_shapes=list(scratch.values()),
        compiler_params=pltpu.CompilerParams(
            collective_id=0, has_side_effects=True, vmem_limit_bytes=63 * 2**20
        ),
    )(counts, images, out_grad, packed, *weights)


def on_device(
    images,
    counts,
    first_gain,
    first_shift,
    query_weight,
    query_bias,
    key_weight,
    value_weight,
    value_bias,
    out_weight,
    out_bias,
    second_gain,
    second_shift,
    up_weight,
    up_bias,
    down_weight,
    down_bias,
    clip_tau,
    out_grad,
):
    part, width = images.shape[2:]
    dps = lax.axis_size("dp")
    dp_at = lax.axis_index("dp")
    shard = query_weight.shape[0]
    pad = (part + 15) // 16 * 16
    size = {
        "width": width,
        "shard": shard,
        "part": part,
        "pad": pad,
        "rows": pad * lax.axis_size("mp"),
        "dps": dps,
        "lines": dps // 2,
        "heads": query_weight.shape[1] // HD,
        "chunks": up_weight.shape[1] // TILE,
        "own_vectors": shard == 128,
    }
    bias_cols = query_bias.shape[1]
    parts = [first_gain, first_shift, out_bias, second_gain, second_shift, down_bias, up_bias[0]]
    if size["own_vectors"]:
        place = jnp.zeros((2, TILE), F32)
        biases = jnp.concatenate([query_bias, value_bias]).astype(F32)
        place = lax.dynamic_update_slice(place, biases, (0, dp_at * bias_cols))
        packed = jnp.concatenate(
            [
                jnp.stack(parts).astype(F32),
                jnp.zeros((1, 128), F32),
                place.reshape(4, 128),
                jnp.zeros((4, 128), F32),
            ]
        )
    else:
        whole = [lax.all_gather(one, "dp", axis=0, tiled=True) for one in parts]
        rest = [
            jnp.pad(lax.all_gather(one[0], "dp", axis=0, tiled=True), (0, width - TILE))
            for one in (query_bias, value_bias)
        ]
        filler = jnp.zeros((width,), BF16)
        packed = jnp.stack(whole + [filler] + rest + [filler] * 6).astype(F32)
    weights = (query_weight, key_weight, value_weight, out_weight, up_weight, down_weight)
    outs = fused_layer(size, counts, images, out_grad, packed, weights)
    result, input_grad, query_g, key_g, value_g, out_g, up_g, down_g, vector_g = outs
    if size["own_vectors"]:
        vectors = [vector_g[row] for row in range(7)]
        start = lax.rem(dp_at * bias_cols, 128)
        query_bias_g = lax.dynamic_slice(vector_g, (DQB, start), (1, bias_cols))
        value_bias_g = lax.dynamic_slice(vector_g, (DVB, start), (1, bias_cols))
        peaks = vector_g[PEAK, : size["heads"]]
    else:
        mine = vector_g[:DUB]
        mine = lax.psum(mine, "mp")
        mine = lax.psum_scatter(mine, "dp", scatter_dimension=1, tiled=True)
        up_bias_g = lax.psum_scatter(vector_g[DUB], "dp", scatter_dimension=0, tiled=True)
        vectors = [mine[row] for row in range(6)] + [up_bias_g]
        both = vector_g[DQB : DVB + 1, :TILE]
        both = lax.psum_scatter(both, "dp", scatter_dimension=1, tiled=True)
        query_bias_g, value_bias_g = both[0:1], both[1:2]
        peaks = lax.pmax(vector_g[PEAK, : size["heads"]], "dp")
    head_root = jnp.sqrt(clip_tau / jnp.maximum(peaks, clip_tau))
    column_root = jnp.repeat(head_root, HD)
    clipped_query = query_weight.astype(F32) * column_root[None, :]
    clipped_key = key_weight.astype(F32) * column_root[None, :]
    bias_root = lax.dynamic_slice(column_root, (dp_at * bias_cols,), (bias_cols,))
    clipped_bias = query_bias.astype(F32) * bias_root[None, :]
    return (
        result,
        input_grad,
        vectors[DG1],
        vectors[DS1],
        query_g,
        query_bias_g,
        key_g,
        value_g,
        value_bias_g,
        out_g,
        vectors[DOB],
        vectors[DG2],
        vectors[DS2],
        up_g,
        vectors[DUB][None, :],
        down_g,
        vectors[DDB],
        peaks,
        clipped_query,
        clipped_key,
        clipped_bias,
    )


def solution(mesh):
    rows = P(None, "dp", "mp", None)
    wide, small, bias = P("dp", "mp"), P("dp"), P("mp", "dp")
    return jax.shard_map(
        on_device,
        mesh=mesh,
        in_specs=(
            rows,
            P(None, "dp"),
            small,
            small,
            wide,
            bias,
            wide,
            wide,
            bias,
            wide,
            small,
            small,
            small,
            wide,
            bias,
            wide,
            small,
            P(),
            rows,
        ),
        out_specs=(
            rows,
            rows,
            small,
            small,
            wide,
            bias,
            wide,
            wide,
            bias,
            wide,
            small,
            small,
            small,
            wide,
            bias,
            wide,
            small,
            P("mp"),
            wide,
            wide,
            bias,
        ),
        check_vma=False,
    )
```

time: 1400 us -> 257 us (0.18)
  waiting for transfers between devices: 821 us -> 0 us
  blocking collectives: 341 us -> 0 us
  Pallas kernels: 0 us -> 239 us
  matrix products: 145 us -> 0 us
  other arithmetic: 38.5 us -> 3.87 us
  between operations: 21 us -> 1.45 us
    reduce_scatter x14 -> x0, waiting for transfers between devices: 613 us -> none  [the longest x4 108 us: collect_normed(): return lax.psum_scatter(partial_rows, 'mp', scatter_dimension=1, tiled=True)]
    all_gather x11 -> x0, blocking collectives: 255 us -> none  [the longest x1 33.5 us: fetch_forward(): lax.all_gather(out_weight, 'dp', axis=0, tiled=True)]
    pallas_call x0 -> x1, Pallas kernels: none -> 239 us  [fused_layer(): pl.pallas_call(functools.partial(layer_kernel, size, names), out_shape=[j...]
    dot_general x48 -> x0, matrix products: 145 us -> none  [the longest x2 20.1 us: on_device(): jnp.einsum('sqhc,skhc->shqk', mixed_back, value_heads, preferred_element_...]
    all_gather x10 -> x0, waiting for transfers between devices: 121 us -> none  [the longest x4 52.2 us: spread_grads(): return lax.all_gather(rows_low, 'mp', axis=1, tiled=True)]
    unnamed x30 -> x0, waiting for transfers between devices: 87.7 us -> none
    unnamed x2 -> x0, blocking collectives: 57.4 us -> none
    pmax x1 -> x0, blocking collectives: 21.6 us -> none  [on_device(): peak_now = jnp.maximum(peak_now, lax.pmax(peak_micro, 'dp'))]
  transfers between devices with their start and end apart: 27 -> 0, of which waited for: 21 -> 0; matrix products, arithmetic and copies ran while one was open for 9% -> 0% of each run, Pallas kernels for 0% -> 0%
where the time goes in v1:
time: 257 us; the launch traced here: 256 us
  Pallas kernels  239 us (93%)
  local copies, waits for them, and re-layouts  12 us (5%)
  other arithmetic  3.87 us (2%)
    pallas_call x1, Pallas kernels, fused_layer(): pl.pallas_call(functools.partial(layer_kernel, size, names), out_shape=[j...  239 us
    unnamed x45, local copies, waits for them, and re-layouts  9.97 us

profile of v1, /device:TPU:0, one launch (start us, length us, event | category | flops | bytes accessed | tf_op | source)
XLA Modules:
  0.0 256.1 jit_solution(3692337266416886432)
XLA Ops:
  0.7 0.0 copy-start.10
  0.7 0.0 copy-start.9
  0.7 1.3 copy.40.refs_0_
  2.0 0.0 copy-done.10
  2.0 0.0 copy-done.9
  2.0 0.2 dynamic_update_slice.3
  2.2 0.0 copy-start.14
  2.2 0.0 copy-start.15
  2.2 0.0 copy-start.16
  2.2 0.0 copy-start.17
  2.3 0.0 copy-start.11
  2.3 0.0 copy-start.12
  2.3 0.0 copy-start.13
  2.3 0.6 copy-done.14
  2.9 0.0 copy-done.15
  2.9 0.0 copy-done.16
  2.9 0.0 copy-done.17
  2.9 0.0 copy-done.11
  2.9 0.0 copy-done.12
  2.9 0.0 copy-done.13
  3.0 0.1 pad.3.clone
  3.1 0.1 pad.1.clone
  3.1 0.7 maximum_maximum_fusion.refs_3_
  3.8 0.0 copy-start.4
  3.8 238.8 %shard_map.346 = (bf16[2,1,152,1024]{3,2,1,0:T(8,128)(2,1)}, bf16[2,1,152,1024]{3,2,1,0:T(8,128)(2,1)}, f32[128,256]{1,0:T(8,128)}, f32[128,256]{1,0:T(8,128)}, ...) custom-call(s32[2,1]{1,0:T(2,128)} %copy.40.refs_0_, ...), custom_call_target="tpu_custom_call" | custom-call | tf_op jit(solution)/shard_map/pallas_call | solution.py:840
  242.7 0.0 copy-start.3
  242.7 1.5 slice_bitcast_fusion.1
  244.8 1.2 divide_sqrt_fusion
  246.0 0.1 broadcast_in_dim.18
  246.1 0.1 mul.25
  246.2 1.3 constant_dynamic-slice_fusion
  247.4 0.0 copy-done.4
  247.4 0.0 copy-done.3
  247.4 0.7 convert_multiply_fusion
  248.2 0.0 copy-start
  248.2 2.0 copy.51
  250.2 0.0 copy-done
  250.2 0.0 copy-start.8
  250.2 0.0 copy-start.7
  250.2 0.0 copy-start.6
  250.2 0.8 copy.52
  251.0 0.2 copy-done.8
  251.2 0.0 copy-start.2
  251.2 0.7 copy.53
  251.8 0.0 copy-done.7
  251.8 0.7 copy.54
  252.5 0.0 copy-done.6
  252.5 0.0 copy-start.5
  252.5 0.7 copy.55
  253.2 0.3 copy-done.5
  253.4 0.7 copy.56
  254.1 0.0 copy-done.2
  254.1 0.0 copy-start.1
  254.1 0.8 copy.57
  254.9 0.4 copy-done.1
  255.3 0.8 copy.58
  (6 shorter events, 0.1 us)
Async XLA Ops:
  0.7 1.3 copy-start.10
  0.7 1.3 copy-start.9
  2.2 0.7 copy-start.14
  2.2 0.7 copy-start.15
  2.2 0.7 copy-start.16
  2.2 0.7 copy-start.17
  2.3 0.7 copy-start.11
  2.3 0.7 copy-start.12
  2.3 0.7 copy-start.13
  3.8 243.6 %copy-start.4 = (bf16[128,256]{1,0:T(8,128)(2,1)S(1)}, bf16[128,256]{1,0:T(8,128)(2,1)}, u32[]{:S(2)}) copy-start(bf16[128,256]{1,0:T(8,128)(2,1)} %refs_5_.1) | copy-start | bytes 196612
  242.7 4.8 %copy-start.3 = (bf16[128,256]{1,0:T(8,128)(2,1)S(1)}, bf16[128,256]{1,0:T(8,128)(2,1)}, u32[]{:S(2)}) copy-start(bf16[128,256]{1,0:T(8,128)(2,1)} %refs_4_.1) | copy-start | bytes 196612
  248.2 2.0 copy-start
  250.2 1.0 copy-start.8
  250.2 1.7 copy-start.7
  250.2 2.3 copy-start.6
  251.2 2.9 %copy-start.2 = (f32[128,1024]{1,0:T(8,128)S(1)}, f32[128,1024]{1,0:T(8,128)}, u32[]{:S(2)}) copy-start(f32[128,1024]{1,0:T(8,128)} %get-tuple-element.87) | copy-start | bytes 1572868
  252.5 1.0 copy-start.5
  254.1 1.2 copy-start.1

commit v2 on v1

--- a/solution.py
+++ b/solution.py
@@ -276,7 +276,9 @@
         return (total + far[...].astype(F32))[: self.part]
 
     def summed(self, piece):
-        return self.weights.at[piece] if piece < 4 else self.wide_sums.at[piece - 4]
+        if piece < 4:
+            return self.proj_back.at[: self.width, piece * TILE : (piece + 1) * TILE]
+        return self.wide_sums.at[piece - 4]
 
     def grad_pair(self, piece, line):
         return self.copy(
@@ -296,18 +298,22 @@
             self.line_peer(step),
         )
 
-    def grad_start(self, piece, left, right):
+    def grad_make(self, piece, left, right, send=True):
         out = self.summed(piece)
         lines_in_tile = TILE // (2 * self.shard)
 
         def step(tile, carry):
             cols = pl.ds(pl.multiple_of(tile * TILE, TILE), TILE)
             out[cols, :] = dot_tn(left[:, cols], right).astype(BF16)
-            for at in range(lines_in_tile):
-                self.grad_pair(piece, tile * lines_in_tile + at).start()
+            if send:
+                for at in range(lines_in_tile):
+                    self.grad_pair(piece, tile * lines_in_tile + at).start()
             return carry
 
         lax.fori_loop(0, self.width // TILE, step, 0)
+
+    def grad_send(self, piece):
+        each(0, self.lines, lambda line: self.grad_pair(piece, line).start())
 
     def grad_pass(self, piece):
         def one(step):
@@ -327,11 +333,22 @@
         for step in range(1, self.lines):
             self.grad_line(piece, step).wait_recv()
             total = total + self.line_in[piece, step - 1].astype(F32)
-        if piece < 4:
-            (self.query_g, self.key_g, self.value_g, self.out_g)[piece][...] = total
-        else:
-            which, chunk = (piece - 4) % 2, (piece - 4) // 2
-            (self.up_g, self.down_g)[which][:, chunk * TILE : (chunk + 1) * TILE] = total
+        at = piece if piece < 4 else 4 + self.chunks * ((piece - 4) % 2) + (piece - 4) // 2
+        self.weight_g[:, at * TILE : (at + 1) * TILE] = total
+
+    def clip(self, peaks):
+        root = jnp.sqrt(self.tau[0, 0] / jnp.maximum(peaks, self.tau[0, 0]))
+        head = lax.broadcasted_iota(jnp.int32, (1, TILE), 1) // HD
+        roots = jnp.zeros((1, TILE), F32)
+        for at in range(self.heads):
+            roots = jnp.where(head == at, root[:, at : at + 1], roots)
+        first = (4 + 2 * self.chunks) * TILE
+        mine = self.slot(self.line_at, self.pair_at)
+        for at, piece in enumerate((PQ, PK)):
+            cols = slice(first + at * TILE, first + (at + 1) * TILE)
+            self.weight_g[:, cols] = self.weights[piece, mine, :].astype(F32) * roots
+        bias = self.packed[8:9, :] * roots[:, 0:128] + self.packed[9:10, :] * roots[:, 128:256]
+        return bias
 
     def vector_copy(self, step):
         return self.copy(
@@ -417,10 +434,15 @@
         for step in range(1, 4):
             self.group_copy(step).wait_recv()
             whole = whole + self.group[step, 0:6, :]
+        narrow = jnp.concatenate([total[7:9], self.clip(most), jnp.zeros((5, 128), F32)], axis=0)
+        shift = lax.rem(128 - lax.rem(self.dp_at * 32, 128), 128)
+        narrow = pltpu.roll(narrow, shift, 1)
         self.vector_g[0:6, :] = whole
-        self.vector_g[6:9, :] = total[6:9]
+        self.vector_g[6:7, :] = total[6:7]
+        self.vector_g[7:9, :] = narrow[0:2]
         self.vector_g[9:10, :] = most
-        self.vector_g[10:16, :] = jnp.zeros((6, 128), F32)
+        self.vector_g[10:11, :] = narrow[2:3]
+        self.vector_g[11:16, :] = jnp.zeros((5, 128), F32)
 
     def vector(self, row, start=0, size=None):
         size = self.width if size is None else size
@@ -432,7 +454,7 @@
 
     def mask(self, micro):
         row = self.mp_at * self.part + lax.broadcasted_iota(jnp.int32, (self.part, 1), 0)
-        live = jnp.where(self.counts[micro, 0] > 0, 1.0, 0.0).astype(F32)
+        live = jnp.where(self.counts[micro] > 0, 1.0, 0.0).astype(F32)
         return jnp.where(row < IMG_LEN, live, 0.0)
 
     def put_rows(self, ref, micro, rows):
@@ -462,7 +484,7 @@
 
     def give_result(self, micro):
         rows = self.after_attn[micro] + self.collected(1, micro) + self.vector(DB)
-        self.result[micro, 0] = (self.mask(micro) * rows).astype(BF16)
+        self.rows_g[0, micro, 0] = (self.mask(micro) * rows).astype(BF16)
 
     def second_norm_back(self, micro):
         incoming = self.collected(2, micro)
@@ -481,7 +503,7 @@
         self.add_sum(DG1, sum_rows(incoming * scaled))
         self.add_sum(DS1, sum_rows(incoming))
         rows = self.attn_back[micro] + norm_back(incoming, scaled, inverse, self.vector(G1))
-        self.input_grad[micro, 0] = rows.astype(BF16)
+        self.rows_g[1, micro, 0] = rows.astype(BF16)
 
     def image_rows(self, micro):
         return pl.ds(micro * self.rows, self.rows)
@@ -510,7 +532,7 @@
     def attend(self, micro):
         rows = self.image_rows(micro)
         self.turned[...] = self.values[rows, :].T
-        live = jnp.where(self.counts[micro, 0] > 0, 0.0, -1e30).astype(F32)
+        live = jnp.where(self.counts[micro] > 0, 0.0, -1e30).astype(F32)
 
         def one_head(head, carry):
             query = jnp.where(self.head_columns(head), self.queries[rows, :], jnp.zeros((), BF16))
@@ -654,34 +676,39 @@
         self.take_vectors()
         for micro in (0, 1):
             self.first_norm(micro)
-        for micro in (0, 1):
-            self.project_back(micro)
-        for piece in range(3):
-            self.pass_weight(piece)
+        self.pass_weight(PQ)
+        self.project_back(0)
+        self.project_back(1)
+        self.spread_on(0, 0, self.normed_one)
+        self.pass_weight(PK)
+        self.spread_on(0, 1, self.normed_one)
+        self.pass_weight(PV)
         for piece in range(4, pieces):
             self.send_weight(piece)
-        for micro in (0, 1):
-            self.spread_on(0, micro, self.normed_one)
-        self.pass_weight(3)
         for piece in range(3):
             self.await_weight(piece)
-        waiting = list(range(4, pieces))
-        for micro in (0, 1):
-            self.spread_end(0, micro, self.normed_one)
-            self.project_heads(micro)
-            self.attend(micro)
-            if micro == 0:
-                self.await_weight(PO)
-            else:
-                self.second_norm(0)
-            self.collect(0, micro, self.out_terms)
-            self.spread_on(2, micro, self.proj_back)
-            self.pass_weight(waiting.pop(0))
+        self.spread_end(0, 0, self.normed_one)
+        self.project_heads(0)
+        self.attend(0)
+        self.pass_weight(PO)
+        self.spread_end(0, 1, self.normed_one)
+        self.project_heads(1)
+        self.attend(1)
+        self.pass_weight(4)
+        self.await_weight(PO)
+        self.collect(0, 0, self.out_terms)
+        self.collect(0, 1, self.out_terms)
+        self.pass_weight(5)
+        self.spread_on(2, 0, self.proj_back)
+        self.spread_on(2, 1, self.proj_back)
+        self.second_norm(0)
+        self.pass_weight(6)
+        self.second_norm(1)
+        self.pass_weight(7)
         self.spread_on(1, 0, self.normed_two)
-        self.second_norm(1)
-        self.pass_weight(waiting.pop(0))
-        self.pass_weight(waiting.pop(0))
+        self.pass_weight(8)
         self.spread_on(1, 1, self.normed_two)
+        waiting = list(range(9, pieces))
         for micro in (0, 1):
             self.spread_end(1, micro, self.normed_two)
             self.spread_end(2, micro, self.proj_back)
@@ -689,57 +716,75 @@
             up, down = 4 + 2 * chunk, 5 + 2 * chunk
             self.await_weight(up)
             self.await_weight(down)
-            for micro in (0, 1):
-                self.feed(micro, chunk)
+            self.feed(0, chunk)
+            if waiting:
+                self.pass_weight(waiting.pop(0))
+            self.feed(1, chunk)
+            if waiting:
+                self.pass_weight(waiting.pop(0))
             cols = slice(chunk * TILE, (chunk + 1) * TILE)
-            self.grad_start(up, self.normed_two, self.pre_back[:, cols])
-            self.grad_start(down, self.proj_back, self.activated[:, cols])
-            for _ in range(2):
-                if waiting:
-                    self.pass_weight(waiting.pop(0))
-            if chunk:
-                self.grad_pass(up - 2)
-                self.grad_pass(down - 2)
+            self.grad_make(up, self.normed_two, self.pre_back[:, cols], False)
         self.spread_sent(1)
-        for micro in (0, 1):
-            self.collect(2, micro, self.wide_terms(self.pre_back, 4))
-        self.grad_pass(pieces - 2)
-        self.grad_pass(pieces - 1)
-        for micro in (0, 1):
-            self.collect(1, micro, self.wide_terms(self.activated, 5))
-            self.second_norm_back(micro)
-        for micro in (0, 1):
-            self.spread_on(3, micro, self.attended_back)
-            self.spread_end(3, micro, self.attended_back)
-            self.attend_back(micro)
-            self.collect(3, micro, self.input_terms)
-        for piece in range(4):
-            each(1, self.lines, lambda step: self.weight_pair(piece, step, False).wait_send())
-        self.grad_start(PO, self.attended_back, self.mixed[...])
-        self.grad_start(PQ, self.normed_one, self.queries[...])
-        self.grad_start(PK, self.normed_one, self.keys[...])
-        self.grad_start(PV, self.normed_one, self.values[...])
-        for micro in (0, 1):
-            self.first_norm_back(micro)
+        self.collect(2, 0, self.wide_terms(self.pre_back, 4))
+        for chunk in range(self.chunks):
+            self.grad_send(4 + 2 * chunk)
+        self.collect(2, 1, self.wide_terms(self.pre_back, 4))
+
+        def down_grad(chunk):
+            cols = slice(chunk * TILE, (chunk + 1) * TILE)
+            self.grad_make(5 + 2 * chunk, self.proj_back, self.activated[:, cols])
+
+        down_grad(0)
+        self.second_norm_back(0)
+        self.grad_pass(4)
+        down_grad(1)
+        down_grad(2)
+        self.second_norm_back(1)
+        self.grad_pass(6)
+        down_grad(3)
+        self.grad_pass(8)
+        self.spread_on(3, 0, self.attended_back)
+        self.spread_end(3, 0, self.attended_back)
+        self.attend_back(0)
+        self.spread_on(3, 1, self.attended_back)
+        self.collect(3, 0, self.input_terms)
+        self.grad_pass(10)
+        self.grad_pass(5)
+        self.spread_end(3, 1, self.attended_back)
+        self.spread_sent(2)
+        self.grad_make(PO, self.attended_back, self.mixed[...])
+        self.attend_back(1)
+        self.grad_make(PQ, self.normed_one, self.queries[...])
+        self.grad_make(PK, self.normed_one, self.keys[...])
+        self.grad_make(PV, self.normed_one, self.values[...])
+        self.grad_pass(7)
+        self.collect(3, 1, self.input_terms)
+        self.grad_pass(9)
+        self.grad_pass(11)
+        self.collect(1, 0, self.wide_terms(self.activated, 5))
+        self.grad_pass(PO)
+        self.first_norm_back(0)
+        self.collect(1, 1, self.wide_terms(self.activated, 5))
+        self.first_norm_back(1)
         self.give_vectors()
-        for piece in (PO, PQ, PK, PV):
-            self.grad_pass(piece)
-        for micro in (0, 1):
-            self.give_result(micro)
+        self.grad_pass(PQ)
+        self.give_result(0)
+        self.grad_pass(PK)
+        self.give_result(1)
+        self.grad_pass(PV)
         for piece in range(4, pieces):
             self.grad_end(piece)
         self.end_vectors()
         for piece in (PO, PQ, PK, PV):
             self.grad_end(piece)
-        for kind in (0, 2, 3):
+        for kind in (0, 3):
             self.spread_sent(kind)
         for one in self.late + self.stage_sends[0] + self.stage_sends[1]:
             one.wait_send()
         for piece in range(pieces):
             self.weight_pair(piece, 0, True).wait_send()
             each(1, self.lines, lambda step: self.weight_line(piece, step).wait_send())
-            if piece >= 4:
-                each(1, self.lines, lambda step: self.weight_pair(piece, step, False).wait_send())
+            each(1, self.lines, lambda step: self.weight_pair(piece, step, False).wait_send())
             each(0, self.lines, lambda line: self.grad_pair(piece, line).wait_send())
             each(1, self.lines, lambda step: self.grad_line(piece, step).wait_send())
         if self.own_vectors:
@@ -756,7 +801,7 @@
     Layer(size, named).run()
 
 
-def fused_layer(size, counts, images, out_grad, packed, weights):
+def fused_layer(size, counts, tau, images, out_grad, packed, weights):
     width, shard, part, rows, pad = (size[key] for key in ("width", "shard", "part", "rows", "pad"))
     lines, dps, pieces = size["lines"], size["dps"], 4 + 2 * size["chunks"]
     units = size["chunks"] * TILE
@@ -764,14 +809,8 @@
     anywhere = pl.BlockSpec(memory_space=pl.ANY)
     vector_shape = (16, 128) if size["own_vectors"] else (16, width)
     outputs = {
-        "result": (images.shape, BF16),
-        "input_grad": (images.shape, BF16),
-        "query_g": ((shard, TILE), F32),
-        "key_g": ((shard, TILE), F32),
-        "value_g": ((shard, TILE), F32),
-        "out_g": ((shard, TILE), F32),
-        "up_g": ((shard, units), F32),
-        "down_g": ((shard, units), F32),
+        "rows_g": ((2,) + images.shape, BF16),
+        "weight_g": ((shard, pieces * TILE + 2 * TILE), F32),
         "vector_g": (vector_shape, F32),
     }
     dma = pltpu.SemaphoreType.DMA
@@ -834,19 +873,19 @@
             "m_send": dma((3,)),
             "m_recv": dma((3,)),
         }
-    inputs = ["counts", "images", "out_grad", "packed"]
+    inputs = ["counts", "tau", "images", "out_grad", "packed"]
     inputs += ["query_w", "key_w", "value_w", "out_w", "up_w", "down_w"]
     names = inputs + list(outputs) + list(scratch)
     return pl.pallas_call(
         functools.partial(layer_kernel, size, names),
         out_shape=[jax.ShapeDtypeStruct(*spec) for spec in outputs.values()],
-        in_specs=[pl.BlockSpec(memory_space=pltpu.SMEM)] + [vmem] * 3 + [anywhere] * 6,
+        in_specs=[pl.BlockSpec(memory_space=pltpu.SMEM)] * 2 + [vmem] * 3 + [anywhere] * 6,
         out_specs=[vmem] * len(outputs),
         scratch_shapes=list(scratch.values()),
         compiler_params=pltpu.CompilerParams(
             collective_id=0, has_side_effects=True, vmem_limit_bytes=63 * 2**20
         ),
-    )(counts, images, out_grad, packed, *weights)
+    )(counts, tau, images, out_grad, packed, *weights)
 
 
 def on_device(
@@ -910,14 +949,23 @@
         filler = jnp.zeros((width,), BF16)
         packed = jnp.stack(whole + [filler] + rest + [filler] * 6).astype(F32)
     weights = (query_weight, key_weight, value_weight, out_weight, up_weight, down_weight)
-    outs = fused_layer(size, counts, images, out_grad, packed, weights)
-    result, input_grad, query_g, key_g, value_g, out_g, up_g, down_g, vector_g = outs
+    rows_g, weight_g, vector_g = fused_layer(
+        size, counts.reshape(-1), clip_tau.reshape(1, 1), images, out_grad, packed, weights
+    )
+    columns, units = query_weight.shape[1], up_weight.shape[1]
+    edges = [0, columns, 2 * columns, 3 * columns, 4 * columns]
+    edges += [edges[-1] + units, edges[-1] + 2 * units]
+    query_g, key_g, value_g, out_g, up_g, down_g = (
+        weight_g[:, low:high] for low, high in zip(edges[:-1], edges[1:])
+    )
     if size["own_vectors"]:
         vectors = [vector_g[row] for row in range(7)]
-        start = lax.rem(dp_at * bias_cols, 128)
-        query_bias_g = lax.dynamic_slice(vector_g, (DQB, start), (1, bias_cols))
-        value_bias_g = lax.dynamic_slice(vector_g, (DVB, start), (1, bias_cols))
+        query_bias_g = vector_g[DQB : DQB + 1, :bias_cols]
+        value_bias_g = vector_g[DVB : DVB + 1, :bias_cols]
         peaks = vector_g[PEAK, : size["heads"]]
+        clipped_query = weight_g[:, edges[-1] : edges[-1] + columns]
+        clipped_key = weight_g[:, edges[-1] + columns :]
+        clipped_bias = vector_g[PEAK + 1 : PEAK + 2, :bias_cols]
     else:
         mine = vector_g[:DUB]
         mine = lax.psum(mine, "mp")
@@ -928,15 +976,15 @@
         both = lax.psum_scatter(both, "dp", scatter_dimension=1, tiled=True)
         query_bias_g, value_bias_g = both[0:1], both[1:2]
         peaks = lax.pmax(vector_g[PEAK, : size["heads"]], "dp")
-    head_root = jnp.sqrt(clip_tau / jnp.maximum(peaks, clip_tau))
-    column_root = jnp.repeat(head_root, HD)
-    clipped_query = query_weight.astype(F32) * column_root[None, :]
-    clipped_key = key_weight.astype(F32) * column_root[None, :]
-    bias_root = lax.dynamic_slice(column_root, (dp_at * bias_cols,), (bias_cols,))
-    clipped_bias = query_bias.astype(F32) * bias_root[None, :]
+        head_root = jnp.sqrt(clip_tau / jnp.maximum(peaks, clip_tau))
+        column_root = jnp.repeat(head_root, HD)
+        clipped_query = query_weight.astype(F32) * column_root[None, :]
+        clipped_key = key_weight.astype(F32) * column_root[None, :]
+        bias_root = lax.dynamic_slice(column_root, (dp_at * bias_cols,), (bias_cols,))
+        clipped_bias = query_bias.astype(F32) * bias_root[None, :]
     return (
-        result,
-        input_grad,
+        rows_g[0],
+        rows_g[1],
         vectors[DG1],
         vectors[DS1],
         query_g,

time: 257 us -> 215 us (0.84)
  Pallas kernels: 239 us -> 205 us
  local copies, waits for them, and re-layouts: 12 us -> 7.14 us
    pallas_call x1, Pallas kernels: 239 us -> 205 us  [fused_layer(): pl.pallas_call(functools.partial(layer_kernel, size, names), out_shape=[j...]
    unnamed x45 -> x5, local copies, waits for them, and re-layouts: 9.97 us -> 2.52 us
where the time goes in v2:
time: 215 us
  Pallas kernels  205 us (95%)
  local copies, waits for them, and re-layouts  7.14 us (3%)
    pallas_call x1, Pallas kernels, fused_layer(): pl.pallas_call(functools.partial(layer_kernel, size, names), out_shape=[j...  205 us

profile of v2, /device:TPU:0, one launch (start us, length us, event | category | flops | bytes accessed | tf_op | source)
XLA Modules:
  0.0 214.6 jit_solution(15363149472770972871)
XLA Ops:
  1.3 0.1 pad.1.clone
  1.4 0.1 pad.3.clone
  1.5 0.7 maximum_convert_fusion
  2.1 0.8 stack.27
  2.9 0.2 dynamic_update_slice.3
  3.1 0.7 maximum_maximum_fusion.refs_4_
  3.8 204.7 %shard_map.346 = (bf16[2,2,1,152,1024]{4,3,2,1,0:T(8,128)(2,1)}, f32[128,3584]{1,0:T(8,128)}, f32[16,128]{1,0:T(8,128)}) custom-call(s32[2]{0:T(128)} %bitcast.32, f32[1,1]{1,0:T(1,128)} %bitcast.31.refs_1_, bf16[2,1,152,1024]{3,2,1,0:T(8,128)(2,1)} %refs_2_.1, bf16[2,1,152,1024]{3,2,1,0:T(8,128)(2,1)} %refs_3_.1, f32[16,128]{1,0:T(8,128)} %maximum_maximum_fusion.refs_4_, ...), custom_call_target="tpu_custom_call" | custom-call | tf_op jit(solution)/shard_map/pallas_call | solution.py:879
  208.5 0.0 copy-start.1
  208.6 0.0 copy-start
  208.6 2.5 %slice_bitcast_fusion = (bf16[2,1,152,1024]{3,2,1,0:T(8,128)(2,1)}, bf16[2,1,152,1024]{3,2,1,0:T(8,128)(2,1)}) fusion(bf16[2,2,1,152,1024]{4,3,2,1,0:T(8,128)(2,1)} %get-tuple-element.24), kind=kLoop, calls=%fused_computation | loop fusion | bytes 2490368
  211.1 0.0 copy-done.1
  211.1 0.5 slice_bitcast_fusion.2
  211.6 0.5 fusion.2
  212.1 0.5 slice_bitcast_fusion.3
  212.7 0.0 copy-done
  212.7 0.9 fusion
  213.5 1.1 fusion.1
  (4 shorter events, 0.0 us)
Async XLA Ops:
  208.5 2.5 %copy-start.1 = (f32[16,128]{1,0:T(8,128)S(1)}, f32[16,128]{1,0:T(8,128)}, u32[]{:S(2)}) copy-start(f32[16,128]{1,0:T(8,128)} %get-tuple-element.25) | copy-start | bytes 24580
  208.6 4.1 %copy-start = (f32[128,3584]{1,0:T(8,128)S(1)}, f32[128,3584]{1,0:T(8,128)}, u32[]{:S(2)}) copy-start(f32[128,3584]{1,0:T(8,128)} %get-tuple-element.26) | copy-start | bytes 5505028
